TPU v7x, 512 devices: a whole 4x4x16 slice. The times are simulated.
512 devices in a mesh: grid: 64 (over z, x), band: 8 (over y, core).
Axes of the slice: x: 4, y: 4, z: 16, core: 2. Of those that a mesh axis runs over, the one named last changes fastest.
Arguments:
- orbitals: float32 [8, 256, 128, 256], P('band', 'grid'), may hold values from -6 to 6
- potential: float32 [256, 128, 256], P('grid'), may hold values from -1 to 1
- partners: bfloat16 [8, 256, 128, 256], P('band', 'grid'), may hold values from -64 to 64
- owners: int32 [6], replicated, may hold values from 0 to 7, as said below
Outputs:
- filtered: float32 [8, 256, 128, 256], P('band', 'grid')
- intersection: float32 [6, 8], P(None, 'band')
Inputs may be any that keep to these rules, and one draw needn't show every extreme that they name: `owners`: band indices; the same index may appear in several steps.
All inputs are finite; a program needn't handle non-finite values.
Results may differ from a plain program's by a relative error of at most 0.0025.
Values may be sent and summed in bfloat16 or wider, within the bound.
No kernel may reach another device: no remote copies, remote signals or barrier semaphores. Data moves between devices by JAX's collectives and lax.ppermute only.
A program may use at most 64 MiB of HBM per device.

v0:
```python
import jax
import jax.numpy as jnp
from jax import lax
from jax.sharding import PartitionSpec as P

STEPS = 6


CENTER_SHIFT = 5.0
HALF_WIDTH = 4.0
NEAR_WEIGHT = 4.0 / 3.0
FAR_WEIGHT = -1.0 / 12.0


def padded_2(block, sides, width):
    for axis, dim in sides:
        count = lax.axis_size(axis)
        forward = [(i, i + 1) for i in range(count - 1)]
        forward.append((count - 1, 0))
        backward = [(target, source) for source, target in forward]
        low = lax.ppermute(
            lax.slice_in_dim(block, block.shape[dim] - width, None, axis=dim), axis, forward
        )
        high = lax.ppermute(lax.slice_in_dim(block, 0, width, axis=dim), axis, backward)
        block = jnp.concatenate([low, block, high], axis=dim)
    return block


def broadcast(value, axis, source):
    kept = jnp.where(lax.axis_index(axis) == source, value, 0).astype(value.dtype)
    return lax.psum(kept, axis)


def local_hamiltonian(padded, potential):
    center = padded[:, 2:-2]
    laplace = -7.5 * center + NEAR_WEIGHT * (padded[:, 3:-1] + padded[:, 1:-3])
    laplace = laplace + FAR_WEIGHT * (padded[:, 4:] + padded[:, :-4])
    for spatial in (2, 3):
        laplace = laplace + NEAR_WEIGHT * (
            jnp.roll(center, 1, spatial) + jnp.roll(center, -1, spatial)
        )
        laplace = laplace + FAR_WEIGHT * (
            jnp.roll(center, 2, spatial) + jnp.roll(center, -2, spatial)
        )
    return -0.5 * laplace + potential[None] * center


def shards(orbitals, potential, partners, owners):

    def applied(field):
        padded = padded_2(field, (("grid", 1),), 2)
        return local_hamiltonian(padded, potential)

    first = (applied(orbitals) - CENTER_SHIFT * orbitals) / HALF_WIDTH
    filtered = 2.0 * (applied(first) - CENTER_SHIFT * first) / HALF_WIDTH - orbitals
    rounded = filtered.astype(jnp.bfloat16)
    cells_total = orbitals.shape[1] * lax.axis_size("grid") * orbitals.shape[2] * orbitals.shape[3]
    factor = float(cells_total) ** (-0.5)
    partials = []
    for owner_step in range(STEPS):
        block = broadcast(rounded, "band", owners[owner_step])
        partial_value = lax.dot_general(
            block, partners, (((1, 2, 3), (1, 2, 3)), ((), ())), preferred_element_type=jnp.float32
        )
        partial_value = lax.psum(partial_value, "grid")
        partials.append(partial_value)
    combined = jnp.concatenate(partials, 0)
    return (filtered, combined * factor)


def solution(mesh):
    in_specs = (
        P("band", "grid", None, None),
        P("grid", None, None),
        P("band", "grid", None, None),
        P(),
    )
    out_specs = (P("band", "grid", None, None), P(None, "band"))
    return jax.shard_map(shards, mesh=mesh, in_specs=in_specs, out_specs=out_specs, check_vma=False)
```

profile of v0, /device:TPU:8, one launch (start us, length us, event | category | flops | bytes accessed | tf_op | source)
XLA Modules:
  0.0 289.5 jit_solution(15072309505631266232)
XLA Ops:
  7.2 0.0 copy-start
  7.2 0.0 all-reduce.4.cloned.1.call-start
  7.2 1.9 fusion.53
  9.1 13.6 %collective-permute-start = (f32[1,2,128,256]{3,2,1,0:T(8,128)}, f32[1,2,128,256]{3,2,1,0:T(8,128)}, u32[]{:S(2)}, u32[]{:S(2)}) collective-permute-start(f32[1,2,128,256]{3,2,1,0:T(8,128)} %get-tuple-element.43), channel_id=1, source_target_pairs={{8,0},{16,8},{24,16},{32,24},{40,32},{48,40},{56,48},{64,56},{72,6... | collective-permute-start | bytes 786440 | tf_op jit(solution)/shard_map/ppermute | solution.py:24
  22.7 1.9 collective-permute-start.1
  24.7 0.0 copy-done
  24.7 0.8 fusion.58
  25.5 0.9 fusion.60
  26.4 0.2 fusion.59
  26.6 0.1 fusion.55
  26.7 0.9 fusion.57
  27.5 0.0 copy-start.8
  27.5 1.1 fusion.61
  28.7 0.0 copy-done.8
  28.7 0.7 fusion.62
  33.0 3.0 %collective-permute-done.1 = f32[1,2,128,256]{3,2,1,0:T(8,128)} collective-permute-done((f32[1,2,128,256]{3,2,1,0:T(8,128)}, f32[1,2,128,256]{3,2,1,0:T(8,128)}, u32[]{:S(2)}, u32[]{:S(2)}) %collective-permute-start.1) | collective-permute-done | bytes 262176 | tf_op jit(solution)/shard_map/ppermute | solution.py:21
  36.0 0.0 copy-start.5
  36.0 0.0 copy-start.6
  36.0 1.0 constant_dynamic-update-slice_fusion.3
  37.1 0.0 copy-start.2
  37.1 0.0 copy-start.3
  37.1 0.0 copy-start.4
  37.1 0.1 constant_dynamic-update-slice_fusion.1
  37.2 0.0 copy-start.1
  37.2 0.0 collective-permute-done
  37.2 1.1 constant_dynamic-update-slice_fusion
  38.3 0.0 copy-done.5
  38.3 0.0 copy-done.6
  38.3 0.0 copy-done.2
  38.3 0.0 copy-done.3
  38.4 0.2 copy-done.4
  38.5 0.2 copy-done.1
  38.7 1.8 broadcast_multiply_fusion
  40.5 0.1 fusion.49
  40.6 0.1 fusion.51
  40.8 0.1 fusion.48
  40.9 0.1 fusion.46
  41.0 0.2 fusion.50
  41.2 4.3 %collective-permute-start.2 = (f32[1,2,128,256]{3,2,1,0:T(8,128)S(1)}, f32[1,2,128,256]{3,2,1,0:T(8,128)S(1)}, u32[]{:S(2)}, u32[]{:S(2)}) collective-permute-start(f32[1,2,128,256]{3,2,1,0:T(8,128)S(1)} %get-tuple-element.25), channel_id=1, source_target_pairs={{8,0},{16,8},{24,16},{32,24},{40,32},{48,40},{56,48},{64,56},{72,6... | collective-permute-start | bytes 786440 | tf_op jit(solution)/shard_map/ppermute | solution.py:24
  45.5 1.9 collective-permute-start.3
  47.4 0.2 fusion.52
  47.6 2.8 collective-permute-done.2
  50.5 7.4 %collective-permute-done.3 = f32[1,2,128,256]{3,2,1,0:T(8,128)S(1)} collective-permute-done((f32[1,2,128,256]{3,2,1,0:T(8,128)S(1)}, f32[1,2,128,256]{3,2,1,0:T(8,128)S(1)}, u32[]{:S(2)}, u32[]{:S(2)}) %collective-permute-start.3) | collective-permute-done | bytes 262176 | tf_op jit(solution)/shard_map/ppermute | solution.py:21
  57.9 1.8 select_bitcast_fusion.5
  59.7 1.1 select_bitcast_fusion.4
  60.8 0.0 copy-start.7
  60.8 0.0 all-reduce.4.cloned.1.call-update
  60.8 70.2 %all-reduce.4.cloned.1.call-done = (bf16[4,128,256]{2,1,0:T(8,128)(2,1)}, bf16[4,128,256]{2,1,0:T(8,128)(2,1)}, bf16[4,128,256]{2,1,0:T(8,128)(2,1)}, bf16[4,128...) async-done(((bf16[4,128,256]{2,1,0:T(8,128)(2,1)}, bf16[4,128,256]{2,1,0:T(8,128)(2,1)}, bf16[4,128,256]{2,1,0:T(8,128)(2,1)}, ...) | async-done | bytes 1572880 | tf_op jit(solution)/shard_map/psum | solution.py:31
  131.0 0.0 copy-done.7
  131.0 2.4 fusion.20
  133.4 144.8 %all-reduce = (f32[1,1]{0,1:T(1,128)}, f32[1,1]{0,1:T(1,128)}, f32[1,1]{0,1:T(1,128)}, f32[1,1]{0,1:T(1,128)}, f32[1,1]{0,1:T(1,128)}, /*index=5*/f32[1,1]{0,1:T(1,128)}) all-reduce(f32[1,1]{0,1:T(1,128)} %bitcast.4, f32[1,1]{0,1:T(1,128)} %bitcast.7, f32[1,1]{0,1:T(1,128)} %bitcast.10, ...), channel_id=1, replica_groups=mesh['grid'=64,'band'=8] {'grid'}, use_global_device_ids=true, to_apply=%region_1.2 | all-reduce | flops 6 | bytes 48 | tf_op jit(solution)/shard_map/psum | solution.py:65
  278.2 3.9 %concatenate.233 = f32[6,1]{0,1:T(1,128)S(1)} concatenate(f32[1,1]{0,1:T(1,128)} %get-tuple-element.8, f32[1,1]{0,1:T(1,128)} %get-tuple-element.9, f32[1,1]{0,1:T(1,128)} %get-tuple-element.10, f32[1,1]{0,1:T(1,128)} %get-tuple-element.11, f32[1,1]{0,1:T(1,128)} %get-tuple-element.12, f32[1,1]{0,1:T(1,128)} %get-tuple-element.13), dimensions={0} | concatenate | bytes 48 | tf_op jit(solution)/shard_map/concatenate | solution.py:67
  282.1 0.5 broadcast_multiply_fusion.1
  (5 shorter events, 0.1 us)
Async XLA Ops:
  7.2 17.5 %copy-start = (f32[1,4,128,256]{3,2,1,0:T(8,128)S(1)}, f32[1,4,128,256]{3,2,1,0:T(8,128)}, u32[]{:S(2)}) copy-start(f32[1,4,128,256]{3,2,1,0:T(8,128)} %param.4) | copy-start | bytes 1572868
  7.2 123.9 %all-reduce.4.cloned.1.call-start = ((), (), s32[]{:S(2)}) async-start(), calls=%async_computation | async-start | bytes 3145728 | tf_op jit(solution)/shard_map/psum | solution.py:31
  9.1 28.1 %collective-permute-start = (f32[1,2,128,256]{3,2,1,0:T(8,128)}, f32[1,2,128,256]{3,2,1,0:T(8,128)}, u32[]{:S(2)}, u32[]{:S(2)}) collective-permute-start(f32[1,2,128,256]{3,2,1,0:T(8,128)} %get-tuple-element.43), channel_id=1, source_target_pairs={{8,0},{16,8},{24,16},{32,24},{40,32},{48,40},{56,48},{64,56},{72,6... | collective-permute-start | bytes 786440 | tf_op jit(solution)/shard_map/ppermute | solution.py:24
  22.7 13.3 %collective-permute-start.1 = (f32[1,2,128,256]{3,2,1,0:T(8,128)}, f32[1,2,128,256]{3,2,1,0:T(8,128)}, u32[]{:S(2)}, u32[]{:S(2)}) collective-permute-start(f32[1,2,128,256]{3,2,1,0:T(8,128)} %get-tuple-element.44), channel_id=1, source_target_pairs={{0,8},{8,16},{16,24},{24,32},{32,40},{40,48},{48,56},{56,64},{64,7... | collective-permute-start | bytes 786440 | tf_op jit(solution)/shard_map/ppermute | solution.py:21
  27.5 1.1 copy-start.8
  36.0 2.3 copy-start.5
  36.0 2.3 copy-start.6
  37.1 1.3 copy-start.2
  37.1 1.3 copy-start.3
  37.1 1.4 copy-start.4
  37.2 1.5 copy-start.1
  41.2 9.2 %collective-permute-start.2 = (f32[1,2,128,256]{3,2,1,0:T(8,128)S(1)}, f32[1,2,128,256]{3,2,1,0:T(8,128)S(1)}, u32[]{:S(2)}, u32[]{:S(2)}) collective-permute-start(f32[1,2,128,256]{3,2,1,0:T(8,128)S(1)} %get-tuple-element.25), channel_id=1, source_target_pairs={{8,0},{16,8},{24,16},{32,24},{40,32},{48,40},{56,48},{64,56},{72,6... | collective-permute-start | bytes 786440 | tf_op jit(solution)/shard_map/ppermute | solution.py:24
  45.5 12.4 %collective-permute-start.3 = (f32[1,2,128,256]{3,2,1,0:T(8,128)S(1)}, f32[1,2,128,256]{3,2,1,0:T(8,128)S(1)}, u32[]{:S(2)}, u32[]{:S(2)}) collective-permute-start(f32[1,2,128,256]{3,2,1,0:T(8,128)S(1)} %get-tuple-element.26), channel_id=1, source_target_pairs={{0,8},{8,16},{16,24},{24,32},{32,40},{40,48},{48,56},{56,64},{64,7... | collective-permute-start | bytes 786440 | tf_op jit(solution)/shard_map/ppermute | solution.py:21
  60.8 70.3 %copy-start.7 = (bf16[1,4,128,256]{3,2,1,0:T(8,128)(2,1)S(1)}, bf16[1,4,128,256]{3,2,1,0:T(8,128)(2,1)}, u32[]{:S(2)}) copy-start(bf16[1,4,128,256]{3,2,1,0:T(8,128)(2,1)} %param.6) | copy-start | bytes 786436
Sparse Core Ops, SparseCore 0:
  60.9 70.0 all-reduce.3
where the time goes:
time: 290 us; the launch traced here: 289 us
  blocking collectives  145 us (50%)
  waiting for transfers between devices  83.6 us (29%)
  starting transfers between devices  21.7 us (7%)
  between operations  17.9 us (6%)
  local copies, waits for them, and re-layouts  13.9 us (5%)
  other arithmetic  7.54 us (3%)
    psum x1, blocking collectives, shards(): partial_value = lax.psum(partial_value, 'grid')  145 us
    psum x1, waiting for transfers between devices, broadcast(): return lax.psum(kept, axis)  70.2 us
    ppermute x2, starting transfers between devices, padded_2(): lax.ppermute(lax.slice_in_dim(block, 0, width, axis=dim), axis, backward)  17.8 us
    ppermute x2, waiting for transfers between devices, padded_2(): lax.ppermute(lax.slice_in_dim(block, block.shape[dim] - width, None, axis...  10.4 us
  transfers between devices with their start and end apart: 5, of which 4 were waited for; matrix products, arithmetic and copies ran while one was open for 2% of the time, Pallas kernels for 0%

commit v1 on v0

v1 whole, which is shorter than its diff:
```python
import jax
import jax.numpy as jnp
from jax import lax
from jax.experimental import pallas as pl
from jax.experimental.pallas import tpu as pltpu
from jax.sharding import Mesh, PartitionSpec as P

STEPS = 6
ORBS = 8
CELLS = 256 * 128 * 256
FACTOR = float(CELLS) ** -0.5

DIAGONAL = 3.75 - 5.0
NEAR = -0.5 * (4.0 / 3.0) / 4.0
FAR = -0.5 * (-1.0 / 12.0) / 4.0

VMEM = pltpu.VMEM
SMEM = pltpu.SMEM
F32 = jnp.float32


def lateral(plane):
    rows, columns = plane.shape
    near = (
        pltpu.roll(plane, 1, 0)
        + pltpu.roll(plane, rows - 1, 0)
        + pltpu.roll(plane, 1, 1)
        + pltpu.roll(plane, columns - 1, 1)
    )
    far = (
        pltpu.roll(plane, 2, 0)
        + pltpu.roll(plane, rows - 2, 0)
        + pltpu.roll(plane, 2, 1)
        + pltpu.roll(plane, columns - 2, 1)
    )
    return near, far


def local_kernel(field_ref, potential_ref, low_ref, high_ref):
    planes = field_ref.shape[0]
    for z in range(planes):
        center = field_ref[z]
        near, far = lateral(center)
        for offset, weight in ((1, "near"), (2, "far")):
            for other in (z - offset, z + offset):
                if 0 <= other < planes:
                    if weight == "near":
                        near = near + field_ref[other]
                    else:
                        far = far + field_ref[other]
        part = (0.25 * (potential_ref[z] + DIAGONAL)) * center + (NEAR * near + FAR * far)
        half = low_ref if z < 2 else high_ref
        half[z % 2] = center
        half[2 + z % 2] = part


def filter_kernel(low_ref, high_ref, left_ref, right_ref, potential_ref, filtered_ref, rounded_ref, first_ref):
    f0, f1, f2, f3 = low_ref[0], low_ref[1], high_ref[0], high_ref[1]
    first_ref[0] = left_ref[2] + FAR * f0
    first_ref[1] = left_ref[3] + NEAR * f0 + FAR * f1
    first_ref[2] = low_ref[2] + NEAR * left_ref[1] + FAR * left_ref[0]
    first_ref[3] = low_ref[3] + FAR * left_ref[1]
    first_ref[4] = high_ref[2] + FAR * right_ref[0]
    first_ref[5] = high_ref[3] + NEAR * right_ref[0] + FAR * right_ref[1]
    first_ref[6] = right_ref[2] + NEAR * f3 + FAR * f2
    first_ref[7] = right_ref[3] + FAR * f3
    for z in range(4):
        center = first_ref[2 + z]
        near, far = lateral(center)
        near = near + (first_ref[1 + z] + first_ref[3 + z])
        far = far + (first_ref[z] + first_ref[4 + z])
        second = (0.25 * (potential_ref[z] + DIAGONAL)) * center + (NEAR * near + FAR * far)
        own = (low_ref if z < 2 else high_ref)[z % 2]
        filtered = 2.0 * second - own
        filtered_ref[z] = filtered
        rounded_ref[z] = filtered.astype(rounded_ref.dtype)


def products_kernel(rounded_ref, partners_ref, out_ref):
    for j in range(ORBS):
        partner = partners_ref[j].astype(F32)
        for o in range(ORBS):
            product = rounded_ref[o].astype(F32) * partner
            total = jnp.sum(product, axis=0, keepdims=True)
            row = total[:, :128] + total[:, 128:]
            for x in range(4):
                out_ref[x, j, pl.ds(o, 1), :] = row


def owners_kernel(owners_ref, parts_ref, out_ref):
    total = parts_ref[0]
    for k in range(1, parts_ref.shape[0]):
        total = total + parts_ref[k]
    row = lax.broadcasted_iota(jnp.int32, total.shape, 0)
    chosen = jnp.zeros_like(total)
    for s in range(STEPS):
        one = jnp.sum(jnp.where(row == owners_ref[s], total, 0.0), axis=0, keepdims=True)
        chosen = jnp.where(row == s, one, chosen)
    for k in range(out_ref.shape[0]):
        out_ref[k] = chosen


def last_kernel(parts_ref, out_ref):
    total = parts_ref[0]
    for k in range(1, parts_ref.shape[0]):
        total = total + parts_ref[k]
    out_ref[...] = jnp.sum(total, axis=1, keepdims=True)[:STEPS] * FACTOR


def call(kernel, shapes, args, spaces=None, scratch=()):
    spaces = spaces or [VMEM] * len(args)
    return pl.pallas_call(
        kernel,
        out_shape=shapes,
        in_specs=[pl.BlockSpec(memory_space=space) for space in spaces],
        out_specs=jax.tree.map(lambda _: pl.BlockSpec(memory_space=VMEM), shapes),
        scratch_shapes=list(scratch),
        compiler_params=pltpu.CompilerParams(vmem_limit_bytes=32 * 1024 * 1024),
    )(*args)


def shards(orbitals, potential, partners, owners):
    grid, band, layer = ("z", "x"), ("y", "core"), ("x", "y", "core")
    count = lax.axis_size(grid)
    up = [(i, (i + 1) % count) for i in range(count)]
    down = [(i, (i - 1) % count) for i in range(count)]
    _, planes, rows, columns = orbitals.shape
    shape = jax.ShapeDtypeStruct
    slab = shape((4, rows, columns), F32)

    low, high = call(local_kernel, (slab, slab), (orbitals[0], potential))
    left = lax.ppermute(high, grid, up)
    right = lax.ppermute(low, grid, down)
    pieces = (ORBS, planes * rows // ORBS, columns)
    partners = lax.all_to_all(partners.reshape(pieces), band, 0, 0, tiled=True)
    filtered, rounded = call(
        filter_kernel,
        (shape((planes, rows, columns), F32), shape((planes, rows, columns), jnp.bfloat16)),
        (low, high, left, right, potential),
        scratch=(pltpu.VMEM((8, rows, columns), F32),),
    )
    rounded = lax.all_to_all(rounded.reshape(pieces), band, 0, 0, tiled=True)
    parts = call(products_kernel, shape((4, ORBS, ORBS, 128), F32), (rounded, partners))
    parts = lax.all_to_all(parts.reshape(4 * ORBS, ORBS, 128), layer, 0, 0, tiled=True)
    depth = lax.axis_size("z")
    parts = call(owners_kernel, shape((depth, ORBS, 128), F32), (owners, parts), (SMEM, VMEM))
    parts = lax.all_to_all(parts, "z", 0, 0, tiled=True)
    intersection = call(last_kernel, shape((STEPS, 1), F32), (parts,))
    return filtered[None], intersection


def solution(mesh):
    fine = Mesh(mesh.devices.reshape(16, 4, 4, 2), ("z", "x", "y", "core"))
    grid, band = ("z", "x"), ("y", "core")
    in_specs = (P(band, grid, None, None), P(grid, None, None), P(band, grid, None, None), P())
    out_specs = (P(band, grid, None, None), P(None, band))
    return jax.shard_map(shards, mesh=fine, in_specs=in_specs, out_specs=out_specs, check_vma=False)
```

time: 290 us -> 80 us (0.28)
  the two profiles are of different devices: /device:TPU:8 before, /device:TPU:1 now
where the time goes in v1:
time: 80 us; the launch traced here: 79.5 us
  blocking collectives  46.2 us (58%)
  starting transfers between devices  21.6 us (27%)
  waiting for transfers between devices  5.14 us (6%)
  Pallas kernels  3.15 us (4%)
  local copies, waits for them, and re-layouts  2.69 us (3%)
    all_to_all x1, blocking collectives, shards(): parts = lax.all_to_all(parts, 'z', 0, 0, tiled=True)  22.5 us
    all_to_all x1, blocking collectives, shards(): rounded = lax.all_to_all(rounded.reshape(pieces), band, 0, 0, tiled=True)  12.3 us
    ppermute x1, starting transfers between devices, shards(): right = lax.ppermute(low, grid, down)  12.1 us
    all_to_all x1, blocking collectives, shards(): lax.all_to_all(parts.reshape(4 * ORBS, ORBS, 128), layer, 0, 0, tiled=True)  11.5 us
    all_to_all x1, starting transfers between devices, shards(): partners = lax.all_to_all(partners.reshape(pieces), band, 0, 0, tiled=True)  5.43 us
    ppermute x1, waiting for transfers between devices, shards(): left = lax.ppermute(high, grid, up)  4.27 us
    ppermute x1, starting transfers between devices, shards(): left = lax.ppermute(high, grid, up)  4.08 us
    pallas_call x5, Pallas kernels, call(): pl.pallas_call(kernel, out_shape=shapes, in_specs=[pl.BlockSpec(memory_sp...  3.15 us
  transfers between devices with their start and end apart: 3, of which 2 were waited for; matrix products, arithmetic and copies ran while one was open for 0% of the time, Pallas kernels for 2%

profile of v1, /device:TPU:1, one launch (start us, length us, event | category | flops | bytes accessed | tf_op | source)
XLA Modules:
  0.0 79.5 jit_solution(1153516103893251042)
XLA Ops:
  0.6 0.0 copy-start
  0.6 1.0 %copy-done = f32[4,128,256]{2,1,0:T(8,128)S(1)} copy-done((f32[4,128,256]{2,1,0:T(8,128)S(1)}, f32[4,128,256]{2,1,0:T(8,128)}, u32[]{:S(2)}) %copy-start) | copy-done | bytes 524312
  1.7 0.0 copy-start.2
  1.7 1.0 %copy-done.2 = f32[1,4,128,256]{3,2,1,0:T(8,128)S(1)} copy-done((f32[1,4,128,256]{3,2,1,0:T(8,128)S(1)}, f32[1,4,128,256]{3,2,1,0:T(8,128)}, u32[]{:S(2)}) %copy-start.2) | copy-done | bytes 524312
  2.7 0.7 shard_map.59
  3.4 0.0 copy-start.1
  3.4 4.1 %collective-permute-start = (f32[4,128,256]{2,1,0:T(8,128)S(1)}, f32[4,128,256]{2,1,0:T(8,128)S(1)}, u32[]{:S(2)}, u32[]{:S(2)}) collective-permute-start(f32[4,128,256]{2,1,0:T(8,128)S(1)} %get-tuple-element.7.high_ref), channel_id=1, source_target_pairs={{0,8},{8,16},{16,24},{24,32},{32,40},{40,48},{48,56},{56,64},{64,7... | collective-permute-start | bytes 1572872 | tf_op jit(solution)/shard_map/ppermute | solution.py:132
  7.5 12.1 %collective-permute-start.1 = (f32[4,128,256]{2,1,0:T(8,128)S(1)}, f32[4,128,256]{2,1,0:T(8,128)S(1)}, u32[]{:S(2)}, u32[]{:S(2)}) collective-permute-start(f32[4,128,256]{2,1,0:T(8,128)S(1)} %get-tuple-element.6.low_ref), channel_id=1, source_target_pairs={{0,504},{8,0},{16,8},{24,16},{32,24},{40,32},{48,40},{56,48},{64,5... | collective-permute-start | bytes 1572872 | tf_op jit(solution)/shard_map/ppermute | solution.py:133
  19.6 5.4 %all-to-all-start.1 = ((bf16[8,64,256]{2,1,0:T(8,128)(2,1)}), bf16[8,64,256]{2,1,0:T(8,128)(2,1)S(1)}, u32[]{:S(2)}, u32[]{:S(2)}) async-start(bf16[8,64,256]{2,1,0:T(8,128)(2,1)} %bitcast.3), calls=%async_computation.1 | async-start | bytes 524288 | tf_op jit(solution)/shard_map/all_to_all | solution.py:135
  25.1 4.3 %collective-permute-done.left_ref = f32[4,128,256]{2,1,0:T(8,128)S(1)} collective-permute-done((f32[4,128,256]{2,1,0:T(8,128)S(1)}, f32[4,128,256]{2,1,0:T(8,128)S(1)}, u32[]{:S(2)}, u32[]{:S(2)}) %collective-permute-start) | collective-permute-done | bytes 524320 | tf_op jit(solution)/shard_map/ppermute | solution.py:132
  29.3 0.9 %collective-permute-done.1.right_ref = f32[4,128,256]{2,1,0:T(8,128)S(1)} collective-permute-done((f32[4,128,256]{2,1,0:T(8,128)S(1)}, f32[4,128,256]{2,1,0:T(8,128)S(1)}, u32[]{:S(2)}, u32[]{:S(2)}) %collective-permute-start.1) | collective-permute-done | bytes 524320 | tf_op jit(solution)/shard_map/ppermute | solution.py:133
  30.2 0.0 copy-done.1
  30.2 1.5 %shard_map.60 = (f32[4,128,256]{2,1,0:T(8,128)}, bf16[4,128,256]{2,1,0:T(8,128)(2,1)S(1)}) custom-call(f32[4,128,256]{2,1,0:T(8,128)S(1)} %get-tuple-element.6.low_ref, f32[4,128,256]{2,1,0:T(8,128)S(1)} %get-tuple-element.7.high_ref, f32[4,128,256]{2,1,0:T(8,128)S(1)} %collective-permute-done.left_ref, f32[4,128,256]{2,1,0:T(8,128)S(1)} %collective-permute-done.1.right_ref, ...), custom_call_target="tpu_custom_call" | custom-call | tf_op jit(solution)/shard_map/pallas_call | solution.py:112
  31.7 0.0 all-to-all-done.1.partners_ref
  31.7 12.3 %all_to_all.20.rounded_ref = bf16[8,64,256]{2,1,0:T(8,128)(2,1)S(1)} all-to-all(bf16[8,64,256]{2,1,0:T(8,128)(2,1)S(1)} %bitcast.7), channel_id=1, replica_groups=mesh['z'=16,'x'=4,'y'=4,'core'=2] {'y','core'}, dimensions={0} | all-to-all | bytes 524288 | tf_op jit(solution)/shard_map/all_to_all | solution.py:142
  44.0 0.3 shard_map.61
  44.3 0.0 copy-start.3
  44.3 11.5 %all_to_all.21.parts_ref = f32[32,8,128]{2,1,0:T(8,128)S(1)} all-to-all(f32[32,8,128]{2,1,0:T(8,128)S(1)} %bitcast.5), channel_id=1, replica_groups=mesh['z'=16,'x'=4,'y'=4,'core'=2] {'x','y','core'}, dimensions={0} | all-to-all | bytes 262144 | tf_op jit(solution)/shard_map/all_to_all | solution.py:144
  55.8 0.0 copy-done.3
  55.8 0.6 shard_map.62
  56.4 22.5 %all_to_all.22.parts_ref = f32[16,8,128]{2,1,0:T(8,128)S(1)} all-to-all(f32[16,8,128]{2,1,0:T(8,128)S(1)} %shard_map.62), channel_id=1, replica_groups=mesh['z'=16,'x'=4,'y'=4,'core'=2] {'z'}, dimensions={0} | all-to-all | bytes 131072 | tf_op jit(solution)/shard_map/all_to_all | solution.py:147
  78.9 0.1 shard_map.63
  78.9 0.6 copy.6
Async XLA Ops:
  0.6 1.0 %copy-start = (f32[4,128,256]{2,1,0:T(8,128)S(1)}, f32[4,128,256]{2,1,0:T(8,128)}, u32[]{:S(2)}) copy-start(f32[4,128,256]{2,1,0:T(8,128)} %potential_ref.3) | copy-start | bytes 1572868
  1.7 1.0 %copy-start.2 = (f32[1,4,128,256]{3,2,1,0:T(8,128)S(1)}, f32[1,4,128,256]{3,2,1,0:T(8,128)}, u32[]{:S(2)}) copy-start(f32[1,4,128,256]{3,2,1,0:T(8,128)} %param.4) | copy-start | bytes 1572868
  3.4 26.8 %copy-start.1 = (f32[4,128,256]{2,1,0:T(8,128)S(1)}, f32[4,128,256]{2,1,0:T(8,128)}, u32[]{:S(2)}) copy-start(f32[4,128,256]{2,1,0:T(8,128)} %potential_ref.3) | copy-start | bytes 1572868
  3.4 25.9 %collective-permute-start = (f32[4,128,256]{2,1,0:T(8,128)S(1)}, f32[4,128,256]{2,1,0:T(8,128)S(1)}, u32[]{:S(2)}, u32[]{:S(2)}) collective-permute-start(f32[4,128,256]{2,1,0:T(8,128)S(1)} %get-tuple-element.7.high_ref), channel_id=1, source_target_pairs={{0,8},{8,16},{16,24},{24,32},{32,40},{40,48},{48,56},{56,64},{64,7... | collective-permute-start | bytes 1572872 | tf_op jit(solution)/shard_map/ppermute | solution.py:132
  7.5 22.7 %collective-permute-start.1 = (f32[4,128,256]{2,1,0:T(8,128)S(1)}, f32[4,128,256]{2,1,0:T(8,128)S(1)}, u32[]{:S(2)}, u32[]{:S(2)}) collective-permute-start(f32[4,128,256]{2,1,0:T(8,128)S(1)} %get-tuple-element.6.low_ref), channel_id=1, source_target_pairs={{0,504},{8,0},{16,8},{24,16},{32,24},{40,32},{48,40},{56,48},{64,5... | collective-permute-start | bytes 1572872 | tf_op jit(solution)/shard_map/ppermute | solution.py:133
  19.6 12.1 %all-to-all-start.1 = ((bf16[8,64,256]{2,1,0:T(8,128)(2,1)}), bf16[8,64,256]{2,1,0:T(8,128)(2,1)S(1)}, u32[]{:S(2)}, u32[]{:S(2)}) async-start(bf16[8,64,256]{2,1,0:T(8,128)(2,1)} %bitcast.3), calls=%async_computation.1 | async-start | bytes 524288 | tf_op jit(solution)/shard_map/all_to_all | solution.py:135
  44.3 11.5 %copy-start.3 = (s32[6]{0:T(128)S(1)}, s32[6]{0:T(128)}, u32[]{:S(2)}) copy-start(s32[6]{0:T(128)} %owners_ref.1) | copy-start | bytes 76

commit v2 on v1

v2 whole, which is shorter than its diff:
```python
import jax
import jax.numpy as jnp
from jax import lax
from jax.experimental import pallas as pl
from jax.experimental.pallas import tpu as pltpu
from jax.sharding import Mesh, PartitionSpec as P

STEPS = 6
ORBS = 8
CELLS = 256 * 128 * 256
FACTOR = float(CELLS) ** -0.5

DIAGONAL = 3.75 - 5.0
NEAR = -0.5 * (4.0 / 3.0) / 4.0
FAR = -0.5 * (-1.0 / 12.0) / 4.0

VMEM = pltpu.VMEM
SMEM = pltpu.SMEM
F32 = jnp.float32
BF16 = jnp.bfloat16


def lateral(plane):
    rows, columns = plane.shape
    near = (
        pltpu.roll(plane, 1, 0)
        + pltpu.roll(plane, rows - 1, 0)
        + pltpu.roll(plane, 1, 1)
        + pltpu.roll(plane, columns - 1, 1)
    )
    far = (
        pltpu.roll(plane, 2, 0)
        + pltpu.roll(plane, rows - 2, 0)
        + pltpu.roll(plane, 2, 1)
        + pltpu.roll(plane, columns - 2, 1)
    )
    return near, far


def split(value):
    high = value.astype(BF16)
    return high, (value - high.astype(F32)).astype(BF16)


def joined(ref, place):
    return ref[place].astype(F32) + ref[place + 1].astype(F32)


def edge(ref, near, far, near_part, far_part):
    ref[0], ref[1] = split(NEAR * near + FAR * far)
    ref[2] = near.astype(BF16)
    ref[3], ref[4] = split(NEAR * near_part + FAR * far_part)
    ref[5] = near_part.astype(BF16)


def local_kernel(field_ref, potential_ref, part_ref, low_ref, high_ref):
    planes = part_ref.shape[0]
    for z in range(planes):
        center = field_ref[z]
        near, far = lateral(center)
        for other in (z - 1, z + 1):
            if 0 <= other < planes:
                near = near + field_ref[other]
        for other in (z - 2, z + 2):
            if 0 <= other < planes:
                far = far + field_ref[other]
        part_ref[z] = (0.25 * (potential_ref[z] + DIAGONAL)) * center + (NEAR * near + FAR * far)
    edge(low_ref, field_ref[0], field_ref[1], part_ref[0], part_ref[1])
    edge(high_ref, field_ref[3], field_ref[2], part_ref[3], part_ref[2])


def find_places(owners_ref, places_ref):
    core = lax.axis_index("core")
    row = lax.broadcasted_iota(jnp.int32, places_ref.shape, 0)
    half = lax.broadcasted_iota(jnp.int32, places_ref.shape, 1) // 64
    places = jnp.full(places_ref.shape, 4, jnp.int32)
    for s in range(STEPS):
        owner = owners_ref[s]
        other = jnp.where(owner % 2 == core, 0, 1)
        places = jnp.where((row == s) & (half == other), owner // 2, places)
    places_ref[...] = places


def filter_kernel(
    owners_ref, field_ref, potential_ref, part_ref, left_ref, right_ref, filtered_ref, rounded_ref, places_ref, first_ref
):
    find_places(owners_ref, places_ref)
    first_ref[0] = part_ref[0] + joined(left_ref, 0)
    first_ref[1] = part_ref[1] + FAR * left_ref[2].astype(F32)
    first_ref[2] = part_ref[2] + FAR * right_ref[2].astype(F32)
    first_ref[3] = part_ref[3] + joined(right_ref, 0)
    f0, f1, f2, f3 = (field_ref[z] for z in range(4))
    outside = (
        joined(left_ref, 3) + ((NEAR * NEAR + FAR * FAR) * f0 + (NEAR * FAR) * f1),
        FAR * (left_ref[5].astype(F32) + (NEAR * f0 + FAR * f1)),
        FAR * (right_ref[5].astype(F32) + (NEAR * f3 + FAR * f2)),
        joined(right_ref, 3) + ((NEAR * NEAR + FAR * FAR) * f3 + (NEAR * FAR) * f2),
    )
    for z in range(4):
        center = first_ref[z]
        near, far = lateral(center)
        for other in (z - 1, z + 1):
            if 0 <= other < 4:
                near = near + first_ref[other]
        for other in (z - 2, z + 2):
            if 0 <= other < 4:
                far = far + first_ref[other]
        second = (0.25 * (potential_ref[z] + DIAGONAL)) * center + (NEAR * near + FAR * far) + outside[z]
        filtered = 2.0 * second - field_ref[z]
        filtered_ref[z] = filtered
        rounded_ref[z] = filtered.astype(BF16)


def products_kernel(own_ref, other_ref, partners_ref, out_ref):
    lane = lax.broadcasted_iota(jnp.int32, (1, 128), 1)
    for place in range(4):
        rows = []
        for rounded_ref in (own_ref, other_ref):
            total = jnp.zeros((8, 128), F32)
            for z in range(own_ref.shape[0]):
                product = rounded_ref[z].astype(F32) * partners_ref[place, z].astype(F32)
                folded = jnp.sum(product.reshape(-1, 8, product.shape[-1]), axis=0)
                total = total + (folded[:, :128] + folded[:, 128:])
            row = jnp.sum(total, axis=0, keepdims=True)
            rows.append(row + pltpu.roll(row, 64, 1))
        both = jnp.where(lane < 64, rows[0], rows[1])
        for x in range(4):
            out_ref[pl.ds(4 * x + place, 1), :] = both


def owners_kernel(places_ref, parts_ref, out_ref):
    total = parts_ref[0:4]
    for x in range(1, 4):
        total = total + parts_ref[4 * x : 4 * x + 4]
    places = places_ref[...]
    chosen = jnp.zeros(places.shape, F32)
    for y in range(4):
        chosen = jnp.where(places == y, total[(y + 2) % 4 : (y + 2) % 4 + 1], chosen)
    sums = jnp.sum(chosen, axis=1, keepdims=True)
    row = lax.broadcasted_iota(jnp.int32, chosen.shape, 0)
    lane = lax.broadcasted_iota(jnp.int32, chosen.shape, 1)
    line = jnp.sum(jnp.where(row == lane, sums, 0.0), axis=0, keepdims=True)
    out_ref[...] = jnp.broadcast_to(line, out_ref.shape)


def last_kernel(parts_ref, out_ref):
    out_ref[...] = jnp.sum(parts_ref[...], axis=0, keepdims=True)[:, :STEPS] * FACTOR


def call(kernel, shapes, args, spaces=None, scratch=(), cost=None):
    spaces = spaces or [VMEM] * len(args)
    return pl.pallas_call(
        kernel,
        out_shape=shapes,
        in_specs=[pl.BlockSpec(memory_space=space) for space in spaces],
        out_specs=jax.tree.map(lambda _: pl.BlockSpec(memory_space=VMEM), shapes),
        scratch_shapes=list(scratch),
        compiler_params=pltpu.CompilerParams(vmem_limit_bytes=8 * 1024 * 1024),
        cost_estimate=cost,
    )(*args)


def from_middle(size, first):
    return [[(first + i) % size for i in range(size)]]


def shards(orbitals, potential, partners, owners):
    grid = ("z", "x")
    count = lax.axis_size(grid)
    up = [(i, (i + 1) % count) for i in range(count)]
    down = [(i, (i - 1) % count) for i in range(count)]
    _, planes, rows, columns = orbitals.shape
    shape = jax.ShapeDtypeStruct
    slab, edges = shape((planes, rows, columns), F32), shape((6, rows, columns), BF16)

    copies = jnp.broadcast_to(partners, (4,) + partners.shape[1:])
    copies, orbitals = lax.optimization_barrier((copies, orbitals))
    part, low, high = call(local_kernel, (slab, edges, edges), (orbitals[0], potential))
    left = lax.ppermute(high, grid, up)
    right = lax.ppermute(low, grid, down)
    partners = lax.all_to_all(copies, "y", 0, 0, tiled=True, axis_index_groups=from_middle(4, 2))
    filtered, rounded, places = call(
        filter_kernel,
        (slab, shape(slab.shape, BF16), shape((ORBS, 128), jnp.int32)),
        (owners, orbitals[0], potential, part, left, right),
        (SMEM,) + (VMEM,) * 5,
        (pltpu.VMEM(slab.shape, F32),),
        cost=pl.CostEstimate(flops=10**11, bytes_accessed=10**6, transcendentals=0),
    )
    other = lax.ppermute(rounded, "core", [(0, 1), (1, 0)])
    parts = call(products_kernel, shape((16, 128), F32), (rounded, other, partners))
    parts = lax.all_to_all(parts, ("x", "y"), 0, 0, tiled=True, axis_index_groups=from_middle(16, 10))
    parts = call(owners_kernel, shape((lax.axis_size("z"), 128), F32), (places, parts))
    parts = lax.all_to_all(parts, "z", 0, 0, tiled=True, axis_index_groups=from_middle(16, 8))
    intersection = call(last_kernel, shape((1, STEPS), F32), (parts,))
    return filtered[None], intersection.T


def solution(mesh):
    fine = Mesh(mesh.devices.reshape(16, 4, 4, 2), ("z", "x", "y", "core"))
    grid, band = ("z", "x"), ("y", "core")
    in_specs = (P(band, grid, None, None), P(grid, None, None), P(band, grid, None, None), P())
    out_specs = (P(band, grid, None, None), P(None, band))
    return jax.shard_map(shards, mesh=fine, in_specs=in_specs, out_specs=out_specs, check_vma=False)
```

time: 80 us -> 64.2 us (0.80)
  the two profiles are of different devices: /device:TPU:1 before, /device:TPU:2 now
where the time goes in v2:
time: 64.2 us; the launch traced here: 63.8 us
  blocking collectives  34.1 us (53%)
  starting transfers between devices  16.4 us (26%)
  waiting for transfers between devices  5.33 us (8%)
  Pallas kernels  5.13 us (8%)
  local copies, waits for them, and re-layouts  2.11 us (3%)
  between operations  0.68 us (1%)
    all_to_all x1, blocking collectives, shards(): lax.all_to_all(parts, ('x', 'y'), 0, 0, tiled=True, axis_index_groups=fro...  19.9 us
    all_to_all x1, blocking collectives, shards(): lax.all_to_all(parts, 'z', 0, 0, tiled=True, axis_index_groups=from_middl...  14.2 us
    ppermute x1, starting transfers between devices, shards(): right = lax.ppermute(low, grid, down)  6.34 us
    pallas_call x5, Pallas kernels, call(): pl.pallas_call(kernel, out_shape=shapes, in_specs=[pl.BlockSpec(memory_sp...  5.13 us
    all_to_all x1, starting transfers between devices, shards(): lax.all_to_all(copies, 'y', 0, 0, tiled=True, axis_index_groups=from_midd...  4.81 us
    ppermute x1, starting transfers between devices, shards(): left = lax.ppermute(high, grid, up)  3.39 us
    all_to_all x1, waiting for transfers between devices, shards(): lax.all_to_all(copies, 'y', 0, 0, tiled=True, axis_index_groups=from_midd...  2.2 us
    broadcast_in_dim x1, local copies, waits for them, and re-layouts, shards(): copies = jnp.broadcast_to(partners, (4,) + partners.shape[1:])  2.1 us
  transfers between devices with their start and end apart: 4, of which 3 were waited for; matrix products, arithmetic and copies ran while one was open for 0% of the time, Pallas kernels for 4%

profile of v2, /device:TPU:2, one launch (start us, length us, event | category | flops | bytes accessed | tf_op | source)
XLA Modules:
  0.0 63.8 jit_solution(2413250415244140854)
XLA Ops:
  0.6 0.0 copy-start
  0.6 0.0 copy-start.1
  0.6 2.1 %broadcast_in_dim.11 = bf16[4,4,128,256]{3,2,1,0:T(8,128)(2,1)} broadcast(bf16[4,128,256]{2,1,0:T(8,128)(2,1)} %bitcast.18), dimensions={1,2,3} | broadcast | bytes 1310720 | tf_op jit(solution)/shard_map/broadcast_in_dim | solution.py:176
  2.8 0.0 copy-done
  2.8 0.0 copy-done.1
  2.8 1.6 %shard_map.59 = (f32[4,128,256]{2,1,0:T(8,128)S(1)}, bf16[6,128,256]{2,1,0:T(8,128)(2,1)}, bf16[6,128,256]{2,1,0:T(8,128)(2,1)}) custom-call(f32[4,128,256]{2,1,0:T(8,128)S(1)} %bitcast.12, f32[4,128,256]{2,1,0:T(8,128)S(1)} %copy-done.1), custom_call_target="tpu_custom_call" | custom-call | tf_op jit(solution)/shard_map/pallas_call | solution.py:152
  4.4 3.4 %collective-permute-start = (bf16[6,128,256]{2,1,0:T(8,128)(2,1)}, bf16[6,128,256]{2,1,0:T(8,128)(2,1)S(1)}, u32[]{:S(2)}, u32[]{:S(2)}) collective-permute-start(bf16[6,128,256]{2,1,0:T(8,128)(2,1)} %get-tuple-element.12), channel_id=1, source_target_pairs={{0,8},{8,16},{16,24},{24,32},{32,40},{40,48},{48,56},{56,64},{64,7... | collective-permute-start | bytes 1179656 | tf_op jit(solution)/shard_map/ppermute | solution.py:179
  7.8 6.3 %collective-permute-start.1 = (bf16[6,128,256]{2,1,0:T(8,128)(2,1)}, bf16[6,128,256]{2,1,0:T(8,128)(2,1)}, u32[]{:S(2)}, u32[]{:S(2)}) collective-permute-start(bf16[6,128,256]{2,1,0:T(8,128)(2,1)} %get-tuple-element.13), channel_id=1, source_target_pairs={{0,504},{8,0},{16,8},{24,16},{32,24},{40,32},{48,40},{56,48},{64,5... | collective-permute-start | bytes 1179656 | tf_op jit(solution)/shard_map/ppermute | solution.py:180
  14.1 4.8 %all-to-all-start = ((bf16[4,4,128,256]{3,2,1,0:T(8,128)(2,1)}), bf16[4,4,128,256]{3,2,1,0:T(8,128)(2,1)S(1)}, u32[]{:S(2)}, u32[]{:S(2)}) async-start(bf16[4,4,128,256]{3,2,1,0:T(8,128)(2,1)} %broadcast_in_dim.11), calls=%async_computation | async-start | bytes 2097152 | tf_op jit(solution)/shard_map/all_to_all | solution.py:181
  19.0 0.0 copy-start.2
  19.0 0.0 collective-permute-done.left_ref
  19.0 1.6 %collective-permute-done.1.right_ref = bf16[6,128,256]{2,1,0:T(8,128)(2,1)} collective-permute-done((bf16[6,128,256]{2,1,0:T(8,128)(2,1)}, bf16[6,128,256]{2,1,0:T(8,128)(2,1)}, u32[]{:S(2)}, u32[]{:S(2)}) %collective-permute-start.1) | collective-permute-done | bytes 393248 | tf_op jit(solution)/shard_map/ppermute | solution.py:180
  20.6 0.0 copy-done.2
  20.6 2.6 %shard_map.60 = (f32[4,128,256]{2,1,0:T(8,128)}, bf16[4,128,256]{2,1,0:T(8,128)(2,1)S(1)}, s32[8,128]{1,0:T(8,128)S(1)}) custom-call(s32[6]{0:T(128)S(1)} %copy-done.2, f32[4,128,256]{2,1,0:T(8,128)S(1)} %bitcast.13, f32[4,128,256]{2,1,0:T(8,128)S(1)} %copy-done.1, f32[4,128,256]{2,1,0:T(8,128)S(1)} %get-tuple-element.11.part_ref, ...), custom_call_target="tpu_custom_call" | custom-call | flops 99999997952 | bytes 1000000 | tf_op jit(solution)/shard_map/pallas_call | solution.py:152
  23.2 1.9 %collective-permute-start.2 = (bf16[4,128,256]{2,1,0:T(8,128)(2,1)S(1)}, bf16[4,128,256]{2,1,0:T(8,128)(2,1)S(1)}, u32[]{:S(2)}, u32[]{:S(2)}) collective-permute-start(bf16[4,128,256]{2,1,0:T(8,128)(2,1)S(1)} %get-tuple-element.16.own_ref), channel_id=1, source_target_pairs={{0,1},{1,0},{2,3},{3,2},{4,5},{5,4},{6,7},{7,6},{8,9},{9,8},{10,11... | collective-permute-start | bytes 786440 | tf_op jit(solution)/shard_map/ppermute | solution.py:190
  25.1 1.5 %collective-permute-done.2.other_ref = bf16[4,128,256]{2,1,0:T(8,128)(2,1)S(1)} collective-permute-done((bf16[4,128,256]{2,1,0:T(8,128)(2,1)S(1)}, bf16[4,128,256]{2,1,0:T(8,128)(2,1)S(1)}, u32[]{:S(2)}, u32[]{:S(2)}) %collective-permute-start.2) | collective-permute-done | bytes 262176 | tf_op jit(solution)/shard_map/ppermute | solution.py:190
  26.6 2.2 %all-to-all-done.partners_ref = bf16[4,4,128,256]{3,2,1,0:T(8,128)(2,1)S(1)} async-done(((bf16[4,4,128,256]{3,2,1,0:T(8,128)(2,1)}), bf16[4,4,128,256]{3,2,1,0:T(8,128)(2,1)S(1)}, u32[]{:S(2)}, u32[]{:S(2)}) %all-to-all-start) | async-done | bytes 1048608 | tf_op jit(solution)/shard_map/all_to_all | solution.py:181
  28.8 0.3 shard_map.61
  29.1 19.9 %all_to_all.27 = f32[16,1,128]{2,1,0:T(1,128)S(1)} all-to-all(f32[16,1,128]{2,1,0:T(1,128)S(1)} %bitcast.14), channel_id=1, replica_groups={{20,22,24,26,28,30,0,2,4,6,8,10,12,14,16,18},{21,23,25,27,29,31,1,3,5,7..., dimensions={0} | all-to-all | bytes 16384 | tf_op jit(solution)/shard_map/all_to_all | solution.py:192
  49.0 0.1 shard_map.62
  49.0 14.2 %all_to_all.28 = f32[16,1,128]{2,1,0:T(1,128)S(1)} all-to-all(f32[16,1,128]{2,1,0:T(1,128)S(1)} %bitcast.16), channel_id=1, replica_groups={{256,288,320,352,384,416,448,480,0,32,64,96,128,160,192,224},{257,289,3..., dimensions={0} | all-to-all | bytes 16384 | tf_op jit(solution)/shard_map/all_to_all | solution.py:194
  63.3 0.5 shard_map.63
Async XLA Ops:
  0.6 2.1 %copy-start = (f32[1,4,128,256]{3,2,1,0:T(8,128)S(1)}, f32[1,4,128,256]{3,2,1,0:T(8,128)}, u32[]{:S(2)}) copy-start(f32[1,4,128,256]{3,2,1,0:T(8,128)} %param.4) | copy-start | bytes 1572868
  0.6 2.1 %copy-start.1 = (f32[4,128,256]{2,1,0:T(8,128)S(1)}, f32[4,128,256]{2,1,0:T(8,128)}, u32[]{:S(2)}) copy-start(f32[4,128,256]{2,1,0:T(8,128)} %potential_ref.3) | copy-start | bytes 1572868
  4.4 14.6 %collective-permute-start = (bf16[6,128,256]{2,1,0:T(8,128)(2,1)}, bf16[6,128,256]{2,1,0:T(8,128)(2,1)S(1)}, u32[]{:S(2)}, u32[]{:S(2)}) collective-permute-start(bf16[6,128,256]{2,1,0:T(8,128)(2,1)} %get-tuple-element.12), channel_id=1, source_target_pairs={{0,8},{8,16},{16,24},{24,32},{32,40},{40,48},{48,56},{56,64},{64,7... | collective-permute-start | bytes 1179656 | tf_op jit(solution)/shard_map/ppermute | solution.py:179
  7.8 12.8 %collective-permute-start.1 = (bf16[6,128,256]{2,1,0:T(8,128)(2,1)}, bf16[6,128,256]{2,1,0:T(8,128)(2,1)}, u32[]{:S(2)}, u32[]{:S(2)}) collective-permute-start(bf16[6,128,256]{2,1,0:T(8,128)(2,1)} %get-tuple-element.13), channel_id=1, source_target_pairs={{0,504},{8,0},{16,8},{24,16},{32,24},{40,32},{48,40},{56,48},{64,5... | collective-permute-start | bytes 1179656 | tf_op jit(solution)/shard_map/ppermute | solution.py:180
  14.1 14.6 %all-to-all-start = ((bf16[4,4,128,256]{3,2,1,0:T(8,128)(2,1)}), bf16[4,4,128,256]{3,2,1,0:T(8,128)(2,1)S(1)}, u32[]{:S(2)}, u32[]{:S(2)}) async-start(bf16[4,4,128,256]{3,2,1,0:T(8,128)(2,1)} %broadcast_in_dim.11), calls=%async_computation | async-start | bytes 2097152 | tf_op jit(solution)/shard_map/all_to_all | solution.py:181
  19.0 1.6 %copy-start.2 = (s32[6]{0:T(128)S(1)}, s32[6]{0:T(128)}, u32[]{:S(2)}) copy-start(s32[6]{0:T(128)} %owners_ref.1) | copy-start | bytes 76
  23.2 3.4 %collective-permute-start.2 = (bf16[4,128,256]{2,1,0:T(8,128)(2,1)S(1)}, bf16[4,128,256]{2,1,0:T(8,128)(2,1)S(1)}, u32[]{:S(2)}, u32[]{:S(2)}) collective-permute-start(bf16[4,128,256]{2,1,0:T(8,128)(2,1)S(1)} %get-tuple-element.16.own_ref), channel_id=1, source_target_pairs={{0,1},{1,0},{2,3},{3,2},{4,5},{5,4},{6,7},{7,6},{8,9},{9,8},{10,11... | collective-permute-start | bytes 786440 | tf_op jit(solution)/shard_map/ppermute | solution.py:190

commit v3 on v2

v3 whole, which is shorter than its diff:
```python
import jax
import jax.numpy as jnp
from jax import lax
from jax.experimental import pallas as pl
from jax.experimental.pallas import tpu as pltpu
from jax.sharding import Mesh, PartitionSpec as P

STEPS = 6
ORBS = 8
CELLS = 256 * 128 * 256
FACTOR = float(CELLS) ** -0.5

DIAGONAL = 3.75 - 5.0
NEAR = -0.5 * (4.0 / 3.0) / 4.0
FAR = -0.5 * (-1.0 / 12.0) / 4.0

VMEM = pltpu.VMEM
SMEM = pltpu.SMEM
F32 = jnp.float32
BF16 = jnp.bfloat16

Z_FIRST = 8
LAYER_FIRST = 21
Y_FIRST = 2


def lateral(plane):
    rows, columns = plane.shape
    near = (
        pltpu.roll(plane, 1, 0)
        + pltpu.roll(plane, rows - 1, 0)
        + pltpu.roll(plane, 1, 1)
        + pltpu.roll(plane, columns - 1, 1)
    )
    far = (
        pltpu.roll(plane, 2, 0)
        + pltpu.roll(plane, rows - 2, 0)
        + pltpu.roll(plane, 2, 1)
        + pltpu.roll(plane, columns - 2, 1)
    )
    return near, far


def store_edge(ref, planes):
    rows = planes[0].shape[0]
    place = lax.broadcasted_iota(jnp.int32, (16, planes[0].shape[1]), 0)
    exponents = jnp.zeros(place.shape, jnp.int32)
    for k, plane in enumerate(planes):
        largest = jnp.maximum(jnp.max(jnp.abs(plane), axis=0, keepdims=True), 1e-30)
        exponent = jnp.floor(jnp.log2(largest)) + 2.0
        ref[pl.ds(k * rows, rows), :] = jnp.round(plane * jnp.exp2(15.0 - exponent)).astype(jnp.int32).astype(jnp.int16)
        exponents = jnp.where(place == k, exponent.astype(jnp.int32), exponents)
    ref[pl.ds(len(planes) * rows, 16), :] = exponents.astype(jnp.int16)


def load_edge(ref, k, rows=128):
    exponent = ref[pl.ds(4 * rows, 16), :].astype(jnp.int32).astype(F32)[k : k + 1]
    return ref[pl.ds(k * rows, rows), :].astype(jnp.int32).astype(F32) * jnp.exp2(exponent - 15.0)


def edge(ref, near, far, near_part, far_part):
    store_edge(ref, (NEAR * near + FAR * far, near, NEAR * near_part + FAR * far_part, near_part))


def local_kernel(field_ref, potential_ref, part_ref, low_ref, high_ref):
    planes = part_ref.shape[0]
    for z in range(planes):
        center = field_ref[z]
        near, far = lateral(center)
        for other in (z - 1, z + 1):
            if 0 <= other < planes:
                near = near + field_ref[other]
        for other in (z - 2, z + 2):
            if 0 <= other < planes:
                far = far + field_ref[other]
        part_ref[z] = (0.25 * (potential_ref[z] + DIAGONAL)) * center + (NEAR * near + FAR * far)
    edge(low_ref, field_ref[0], field_ref[1], part_ref[0], part_ref[1])
    edge(high_ref, field_ref[3], field_ref[2], part_ref[3], part_ref[2])


def member(place, size, first):
    return (first + place) % size


def product_rows(rounded_ref, partners_ref, out_ref):
    for k in range(partners_ref.shape[0]):
        total = jnp.zeros((8, 128), F32)
        for z in range(partners_ref.shape[1]):
            product = rounded_ref[z].astype(F32) * partners_ref[k, z].astype(F32)
            folded = jnp.sum(product.reshape(-1, 8, product.shape[-1]), axis=0)
            total = total + (folded[:, :128] + folded[:, 128:])
        out_ref[pl.ds(k, 1), :] = jnp.sum(total, axis=0, keepdims=True)


def filter_kernel(
    owners_ref, field_ref, potential_ref, part_ref, left_ref, right_ref, partners_ref, filtered_ref, rounded_ref, rows_ref, places_ref, first_ref
):
    row = lax.broadcasted_iota(jnp.int32, places_ref.shape, 0)
    places = jnp.full(places_ref.shape, ORBS, jnp.int32)
    for s in range(STEPS):
        places = jnp.where(row == s, owners_ref[s], places)
    places_ref[...] = places
    first_ref[0] = part_ref[0] + load_edge(left_ref, 0)
    first_ref[1] = part_ref[1] + FAR * load_edge(left_ref, 1)
    first_ref[2] = part_ref[2] + FAR * load_edge(right_ref, 1)
    first_ref[3] = part_ref[3] + load_edge(right_ref, 0)
    f0, f1, f2, f3 = (field_ref[z] for z in range(4))
    outside = (
        load_edge(left_ref, 2) + ((NEAR * NEAR + FAR * FAR) * f0 + (NEAR * FAR) * f1),
        FAR * (load_edge(left_ref, 3) + (NEAR * f0 + FAR * f1)),
        FAR * (load_edge(right_ref, 3) + (NEAR * f3 + FAR * f2)),
        load_edge(right_ref, 2) + ((NEAR * NEAR + FAR * FAR) * f3 + (NEAR * FAR) * f2),
    )
    for z in range(4):
        center = first_ref[z]
        near, far = lateral(center)
        for other in (z - 1, z + 1):
            if 0 <= other < 4:
                near = near + first_ref[other]
        for other in (z - 2, z + 2):
            if 0 <= other < 4:
                far = far + first_ref[other]
        second = (0.25 * (potential_ref[z] + DIAGONAL)) * center + (NEAR * near + FAR * far) + outside[z]
        filtered = 2.0 * second - field_ref[z]
        filtered_ref[z] = filtered
        rounded_ref[z] = filtered.astype(BF16)
    product_rows(rounded_ref, partners_ref, rows_ref)


def products_kernel(rounded_ref, partners_ref, own_ref, out_ref, other_ref):
    product_rows(rounded_ref, partners_ref, other_ref)
    core = lax.axis_index("core")
    own, other = own_ref[...], other_ref[...]
    rows = jnp.where(core == 0, own, other), jnp.where(core == 0, other, own)
    for place in range(out_ref.shape[0]):
        device = member(place, out_ref.shape[0], LAYER_FIRST)
        y = (device // 2 - Y_FIRST) % 4
        out_ref[pl.ds(place, 1), :] = rows[device % 2][y : y + 1]


def owners_kernel(places_ref, parts_ref, out_ref):
    totals = [jnp.zeros((1, 128), F32)] * ORBS
    for place in range(parts_ref.shape[0]):
        owner = member(place, parts_ref.shape[0], LAYER_FIRST) % ORBS
        totals[owner] = totals[owner] + parts_ref[pl.ds(place, 1), :]
    places = places_ref[...]
    chosen = jnp.zeros(places.shape, F32)
    for owner in range(ORBS):
        chosen = jnp.where(places == owner, totals[owner], chosen)
    sums = jnp.sum(chosen, axis=1, keepdims=True)
    row = lax.broadcasted_iota(jnp.int32, chosen.shape, 0)
    lane = lax.broadcasted_iota(jnp.int32, chosen.shape, 1)
    line = jnp.sum(jnp.where(row == lane, sums, 0.0), axis=0, keepdims=True)
    out_ref[...] = jnp.broadcast_to(line, out_ref.shape)


def last_kernel(parts_ref, out_ref):
    out_ref[...] = jnp.sum(parts_ref[...], axis=0, keepdims=True)[:, :STEPS] * FACTOR


def call(kernel, shapes, args, spaces=None, scratch=(), cost=None):
    spaces = spaces or [VMEM] * len(args)
    return pl.pallas_call(
        kernel,
        out_shape=shapes,
        in_specs=[pl.BlockSpec(memory_space=space) for space in spaces],
        out_specs=jax.tree.map(lambda _: pl.BlockSpec(memory_space=VMEM), shapes),
        scratch_shapes=list(scratch),
        compiler_params=pltpu.CompilerParams(vmem_limit_bytes=8 * 1024 * 1024),
        cost_estimate=cost,
    )(*args)


def from_middle(size, first):
    return [[(first + i) % size for i in range(size)]]


def shards(orbitals, potential, partners, owners):
    grid = ("z", "x")
    count = lax.axis_size(grid)
    up = [(i, (i + 1) % count) for i in range(count)]
    down = [(i, (i - 1) % count) for i in range(count)]
    _, planes, rows, columns = orbitals.shape
    shape = jax.ShapeDtypeStruct
    slab, edges = shape((planes, rows, columns), F32), shape((4 * rows + 16, columns), jnp.int16)

    copies = jnp.broadcast_to(partners, (4,) + partners.shape[1:])
    copies, orbitals = lax.optimization_barrier((copies, orbitals))
    partners = lax.all_to_all(copies, "y", 0, 0, tiled=True, axis_index_groups=from_middle(4, Y_FIRST))
    part, low, high = call(local_kernel, (slab, edges, edges), (orbitals[0], potential))
    left = lax.ppermute(high, grid, up)
    right = lax.ppermute(low, grid, down)
    partners, left = lax.optimization_barrier((partners, left))
    others = lax.ppermute(partners, "core", [(0, 1), (1, 0)])
    filtered, rounded, own, places = call(
        filter_kernel,
        (slab, shape(slab.shape, BF16), shape((4, 128), F32), shape((ORBS, 128), jnp.int32)),
        (owners, orbitals[0], potential, part, left, right, partners),
        (SMEM,) + (VMEM,) * 6,
        (pltpu.VMEM(slab.shape, F32),),
        cost=pl.CostEstimate(flops=10**10, bytes_accessed=10**6, transcendentals=0),
    )
    parts = call(products_kernel, shape((4 * ORBS, 128), F32), (rounded, others, own), scratch=(pltpu.VMEM((4, 128), F32),))
    layer = ("x", "y", "core")
    parts = lax.all_to_all(parts, layer, 0, 0, tiled=True, axis_index_groups=from_middle(4 * ORBS, LAYER_FIRST))
    depth = lax.axis_size("z")
    parts = call(owners_kernel, shape((depth, 128), F32), (places, parts))
    parts = lax.all_to_all(parts, "z", 0, 0, tiled=True, axis_index_groups=from_middle(depth, Z_FIRST))
    intersection = call(last_kernel, shape((1, STEPS), F32), (parts,))
    return filtered[None], intersection.T


def solution(mesh):
    fine = Mesh(mesh.devices.reshape(16, 4, 4, 2), ("z", "x", "y", "core"))
    grid, band = ("z", "x"), ("y", "core")
    in_specs = (P(band, grid, None, None), P(grid, None, None), P(band, grid, None, None), P())
    out_specs = (P(band, grid, None, None), P(None, band))
    return jax.shard_map(shards, mesh=fine, in_specs=in_specs, out_specs=out_specs, check_vma=False)
```

time: 64.2 us -> 59.6 us (0.928)
  blocking collectives: 34.1 us -> 32.1 us
  Pallas kernels: 5.13 us -> 3.76 us
  waiting for transfers between devices: 5.33 us -> 4.09 us
    all_to_all x1, blocking collectives: 19.9 us -> 17.3 us  [shards(): lax.all_to_all(parts, layer, 0, 0, tiled=True, axis_index_groups=from_mid...]
    ppermute x1, waiting for transfers between devices: 0.01 us -> 2.48 us  [shards(): left = lax.ppermute(high, grid, up)]
    all_to_all x1, starting transfers between devices: 4.81 us -> 6.81 us  [shards(): lax.all_to_all(copies, 'y', 0, 0, tiled=True, axis_index_groups=from_midd...]
    ppermute x1, starting transfers between devices: 6.34 us -> 4.46 us  [shards(): right = lax.ppermute(low, grid, down)]
    ppermute x1, waiting for transfers between devices: 1.62 us -> 0.01 us  [shards(): right = lax.ppermute(low, grid, down)]
    pallas_call x5, Pallas kernels: 5.13 us -> 3.76 us  [call(): pl.pallas_call(kernel, out_shape=shapes, in_specs=[pl.BlockSpec(memory_sp...]
    ppermute x1, waiting for transfers between devices: 1.5 us -> 0.39 us  [shards(): others = lax.ppermute(partners, 'core', [(0, 1), (1, 0)])]
    all_to_all x1, waiting for transfers between devices: 2.2 us -> 1.21 us  [shards(): lax.all_to_all(copies, 'y', 0, 0, tiled=True, axis_index_groups=from_midd...]
  transfers between devices with their start and end apart: 4 -> 4, of which waited for: 3 -> 3; matrix products, arithmetic and copies ran while one was open for 0% -> 0% of each run, Pallas kernels for 4% -> 5%
where the time goes in v3:
time: 59.6 us; the launch traced here: 59.2 us
  blocking collectives  32.1 us (54%)
  starting transfers between devices  16.6 us (28%)
  waiting for transfers between devices  4.09 us (7%)
  Pallas kernels  3.76 us (6%)
  local copies, waits for them, and re-layouts  2.03 us (3%)
  between operations  0.69 us (1%)
    all_to_all x1, blocking collectives, shards(): lax.all_to_all(parts, layer, 0, 0, tiled=True, axis_index_groups=from_mid...  17.3 us
    all_to_all x1, blocking collectives, shards(): lax.all_to_all(parts, 'z', 0, 0, tiled=True, axis_index_groups=from_middl...  14.7 us
    all_to_all x1, starting transfers between devices, shards(): lax.all_to_all(copies, 'y', 0, 0, tiled=True, axis_index_groups=from_midd...  6.81 us
    ppermute x1, starting transfers between devices, shards(): right = lax.ppermute(low, grid, down)  4.46 us
    pallas_call x5, Pallas kernels, call(): pl.pallas_call(kernel, out_shape=shapes, in_specs=[pl.BlockSpec(memory_sp...  3.76 us
    ppermute x1, starting transfers between devices, shards(): left = lax.ppermute(high, grid, up)  3.4 us
    ppermute x1, waiting for transfers between devices, shards(): left = lax.ppermute(high, grid, up)  2.48 us
    broadcast_in_dim x1, local copies, waits for them, and re-layouts, shards(): copies = jnp.broadcast_to(partners, (4,) + partners.shape[1:])  2.02 us
  transfers between devices with their start and end apart: 4, of which 3 were waited for; matrix products, arithmetic and copies ran while one was open for 0% of the time, Pallas kernels for 5%

profile of v3, /device:TPU:2, one launch (start us, length us, event | category | flops | bytes accessed | tf_op | source)
XLA Modules:
  0.0 59.2 jit_solution(1396840658679749808)
XLA Ops:
  0.6 2.0 %broadcast_in_dim.11 = bf16[4,4,128,256]{3,2,1,0:T(8,128)(2,1)} broadcast(bf16[4,128,256]{2,1,0:T(8,128)(2,1)} %bitcast.18), dimensions={1,2,3} | broadcast | bytes 1310720 | tf_op jit(solution)/shard_map/broadcast_in_dim | solution.py:187
  2.6 0.0 copy-start
  2.6 0.0 copy-start.1
  2.7 6.8 %all-to-all-start = ((bf16[4,4,128,256]{3,2,1,0:T(8,128)(2,1)}), bf16[4,4,128,256]{3,2,1,0:T(8,128)(2,1)S(1)}, u32[]{:S(2)}, u32[]{:S(2)}) async-start(bf16[4,4,128,256]{3,2,1,0:T(8,128)(2,1)} %broadcast_in_dim.11), calls=%async_computation | async-start | bytes 2097152 | tf_op jit(solution)/shard_map/all_to_all | solution.py:189
  9.5 0.0 copy-done
  9.5 0.0 copy-done.1
  9.5 0.8 %shard_map.59 = (f32[4,128,256]{2,1,0:T(8,128)S(1)}, s16[528,256]{1,0:T(8,128)(2,1)S(1)}, s16[528,256]{1,0:T(8,128)(2,1)S(1)}) custom-call(f32[4,128,256]{2,1,0:T(8,128)S(1)} %bitcast.12, f32[4,128,256]{2,1,0:T(8,128)S(1)} %copy-done.1), custom_call_target="tpu_custom_call" | custom-call | tf_op jit(solution)/shard_map/pallas_call | solution.py:163
  10.3 3.4 %collective-permute-start = (s16[528,256]{1,0:T(8,128)(2,1)S(1)}, s16[528,256]{1,0:T(8,128)(2,1)S(1)}, u32[]{:S(2)}, u32[]{:S(2)}) collective-permute-start(s16[528,256]{1,0:T(8,128)(2,1)S(1)} %get-tuple-element.16), channel_id=1, source_target_pairs={{0,8},{8,16},{16,24},{24,32},{32,40},{40,48},{48,56},{56,64},{64,7... | collective-permute-start | bytes 811016 | tf_op jit(solution)/shard_map/ppermute | solution.py:191
  13.7 0.0 copy-start.2
  13.7 4.5 %collective-permute-start.1 = (s16[528,256]{1,0:T(8,128)(2,1)S(1)}, s16[528,256]{1,0:T(8,128)(2,1)S(1)}, u32[]{:S(2)}, u32[]{:S(2)}) collective-permute-start(s16[528,256]{1,0:T(8,128)(2,1)S(1)} %get-tuple-element.18), channel_id=1, source_target_pairs={{0,504},{8,0},{16,8},{24,16},{32,24},{40,32},{48,40},{56,48},{64,5... | collective-permute-start | bytes 811016 | tf_op jit(solution)/shard_map/ppermute | solution.py:192
  18.2 2.5 %collective-permute-done.left_ref = s16[528,256]{1,0:T(8,128)(2,1)S(1)} collective-permute-done((s16[528,256]{1,0:T(8,128)(2,1)S(1)}, s16[528,256]{1,0:T(8,128)(2,1)S(1)}, u32[]{:S(2)}, u32[]{:S(2)}) %collective-permute-start) | collective-permute-done | bytes 270368 | tf_op jit(solution)/shard_map/ppermute | solution.py:191
  20.7 1.2 %all-to-all-done.partners_ref = bf16[4,4,128,256]{3,2,1,0:T(8,128)(2,1)S(1)} async-done(((bf16[4,4,128,256]{3,2,1,0:T(8,128)(2,1)}), bf16[4,4,128,256]{3,2,1,0:T(8,128)(2,1)S(1)}, u32[]{:S(2)}, u32[]{:S(2)}) %all-to-all-start) | async-done | bytes 1048608 | tf_op jit(solution)/shard_map/all_to_all | solution.py:189
  21.9 1.9 %collective-permute-start.2 = (bf16[4,4,128,256]{3,2,1,0:T(8,128)(2,1)S(1)}, bf16[4,4,128,256]{3,2,1,0:T(8,128)(2,1)S(1)}, u32[]{:S(2)}, u32[]{:S(2)}) collective-permute-start(bf16[4,4,128,256]{3,2,1,0:T(8,128)(2,1)S(1)} %all-to-all-done.partners_ref), channel_id=1, source_target_pairs={{0,1},{1,0},{2,3},{3,2},{4,5},{5,4},{6,7},{7,6},{8,9},{9,8},{10,11... | collective-permute-start | bytes 3145736 | tf_op jit(solution)/shard_map/ppermute | solution.py:194
  23.8 0.0 collective-permute-done.1.right_ref
  23.8 0.0 copy-done.2
  23.8 2.2 %shard_map.60 = (f32[4,128,256]{2,1,0:T(8,128)}, bf16[4,128,256]{2,1,0:T(8,128)(2,1)S(1)}, f32[4,128]{1,0:T(4,128)S(1)}, s32[8,128]{1,0:T(8,128)S(1)}) custom-call(s32[6]{0:T(128)S(1)} %copy-done.2, f32[4,128,256]{2,1,0:T(8,128)S(1)} %bitcast.13, f32[4,128,256]{2,1,0:T(8,128)S(1)} %copy-done.1, f32[4,128,256]{2,1,0:T(8,128)S(1)} %get-tuple-element.14.part_ref, ...), custom_call_target="tpu_custom_call" | custom-call | flops 10000000000 | bytes 1000000 | tf_op jit(solution)/shard_map/pallas_call | solution.py:163
  26.0 0.4 collective-permute-done.2.partners_ref
  26.4 0.1 shard_map.61
  26.5 17.3 %all_to_all.27 = f32[32,1,128]{2,1,0:T(1,128)S(1)} all-to-all(f32[32,1,128]{2,1,0:T(1,128)S(1)} %bitcast.15), channel_id=1, replica_groups={{21,22,23,24,25,26,27,28,29,30,31,0,1,2,3,4,5,6,7,8,9,10,11,12,13,14,15..., dimensions={0} | all-to-all | bytes 32768 | tf_op jit(solution)/shard_map/all_to_all | solution.py:205
  43.9 0.1 shard_map.62
  44.0 14.7 %all_to_all.28 = f32[16,1,128]{2,1,0:T(1,128)S(1)} all-to-all(f32[16,1,128]{2,1,0:T(1,128)S(1)} %bitcast.16), channel_id=1, replica_groups={{256,288,320,352,384,416,448,480,0,32,64,96,128,160,192,224},{257,289,3..., dimensions={0} | all-to-all | bytes 16384 | tf_op jit(solution)/shard_map/all_to_all | solution.py:208
  58.7 0.5 shard_map.63
Async XLA Ops:
  2.6 6.8 %copy-start = (f32[1,4,128,256]{3,2,1,0:T(8,128)S(1)}, f32[1,4,128,256]{3,2,1,0:T(8,128)}, u32[]{:S(2)}) copy-start(f32[1,4,128,256]{3,2,1,0:T(8,128)} %param.4) | copy-start | bytes 1572868
  2.6 6.8 %copy-start.1 = (f32[4,128,256]{2,1,0:T(8,128)S(1)}, f32[4,128,256]{2,1,0:T(8,128)}, u32[]{:S(2)}) copy-start(f32[4,128,256]{2,1,0:T(8,128)} %potential_ref.3) | copy-start | bytes 1572868
  2.7 19.2 %all-to-all-start = ((bf16[4,4,128,256]{3,2,1,0:T(8,128)(2,1)}), bf16[4,4,128,256]{3,2,1,0:T(8,128)(2,1)S(1)}, u32[]{:S(2)}, u32[]{:S(2)}) async-start(bf16[4,4,128,256]{3,2,1,0:T(8,128)(2,1)} %broadcast_in_dim.11), calls=%async_computation | async-start | bytes 2097152 | tf_op jit(solution)/shard_map/all_to_all | solution.py:189
  10.3 10.4 %collective-permute-start = (s16[528,256]{1,0:T(8,128)(2,1)S(1)}, s16[528,256]{1,0:T(8,128)(2,1)S(1)}, u32[]{:S(2)}, u32[]{:S(2)}) collective-permute-start(s16[528,256]{1,0:T(8,128)(2,1)S(1)} %get-tuple-element.16), channel_id=1, source_target_pairs={{0,8},{8,16},{16,24},{24,32},{32,40},{40,48},{48,56},{56,64},{64,7... | collective-permute-start | bytes 811016 | tf_op jit(solution)/shard_map/ppermute | solution.py:191
  13.7 10.1 %copy-start.2 = (s32[6]{0:T(128)S(1)}, s32[6]{0:T(128)}, u32[]{:S(2)}) copy-start(s32[6]{0:T(128)} %owners_ref.1) | copy-start | bytes 76
  13.7 10.1 %collective-permute-start.1 = (s16[528,256]{1,0:T(8,128)(2,1)S(1)}, s16[528,256]{1,0:T(8,128)(2,1)S(1)}, u32[]{:S(2)}, u32[]{:S(2)}) collective-permute-start(s16[528,256]{1,0:T(8,128)(2,1)S(1)} %get-tuple-element.18), channel_id=1, source_target_pairs={{0,504},{8,0},{16,8},{24,16},{32,24},{40,32},{48,40},{56,48},{64,5... | collective-permute-start | bytes 811016 | tf_op jit(solution)/shard_map/ppermute | solution.py:192
  21.9 4.5 %collective-permute-start.2 = (bf16[4,4,128,256]{3,2,1,0:T(8,128)(2,1)S(1)}, bf16[4,4,128,256]{3,2,1,0:T(8,128)(2,1)S(1)}, u32[]{:S(2)}, u32[]{:S(2)}) collective-permute-start(bf16[4,4,128,256]{3,2,1,0:T(8,128)(2,1)S(1)} %all-to-all-done.partners_ref), channel_id=1, source_target_pairs={{0,1},{1,0},{2,3},{3,2},{4,5},{5,4},{6,7},{7,6},{8,9},{9,8},{10,11... | collective-permute-start | bytes 3145736 | tf_op jit(solution)/shard_map/ppermute | solution.py:194

commit v4 on v3

v4 whole, which is shorter than its diff:
```python
import jax
import jax.numpy as jnp
from jax import lax
from jax.experimental import pallas as pl
from jax.experimental.pallas import tpu as pltpu
from jax.sharding import Mesh, PartitionSpec as P

STEPS = 6
ORBS = 8
CELLS = 256 * 128 * 256
FACTOR = float(CELLS) ** -0.5

DIAGONAL = 3.75 - 5.0
NEAR = -0.5 * (4.0 / 3.0) / 4.0
FAR = -0.5 * (-1.0 / 12.0) / 4.0

VMEM = pltpu.VMEM
SMEM = pltpu.SMEM
F32 = jnp.float32
BF16 = jnp.bfloat16

ROWS = 32

Z_FIRST = 8
LAYER_FIRST = 21
Y_FIRST = 0


def lateral(ref, z, start, count):
    rows, columns = ref.shape[1:]
    if start == 0:
        wide = jnp.concatenate([ref[z, rows - 8 : rows], ref[z, 0 : count + 8]], axis=0)
    elif start + count == rows:
        wide = jnp.concatenate([ref[z, start - 8 : rows], ref[z, 0:8]], axis=0)
    else:
        wide = ref[z, start - 8 : start + count + 8]
    center = wide[8 : 8 + count]
    near = pltpu.roll(center, 1, 1) + pltpu.roll(center, columns - 1, 1)
    far = pltpu.roll(center, 2, 1) + pltpu.roll(center, columns - 2, 1)
    near = near + (pltpu.roll(wide, 1, 0)[8 : 8 + count] + pltpu.roll(wide, count + 15, 0)[8 : 8 + count])
    far = far + (pltpu.roll(wide, 2, 0)[8 : 8 + count] + pltpu.roll(wide, count + 14, 0)[8 : 8 + count])
    return center, near, far


def stencil(ref, potential_ref, z, start, count):
    block = pl.ds(start, count)
    center, near, far = lateral(ref, z, start, count)
    for other in (z - 1, z + 1):
        if 0 <= other < ref.shape[0]:
            near = near + ref[other, block]
    for other in (z - 2, z + 2):
        if 0 <= other < ref.shape[0]:
            far = far + ref[other, block]
    return (0.25 * (potential_ref[z, block] + DIAGONAL)) * center + (NEAR * near + FAR * far)


def store_edge(ref, planes):
    rows = planes[0].shape[0]
    place = lax.broadcasted_iota(jnp.int32, (16, planes[0].shape[1]), 0)
    exponents = jnp.zeros(place.shape, jnp.int32)
    for k, plane in enumerate(planes):
        largest = jnp.maximum(jnp.max(jnp.abs(plane), axis=0, keepdims=True), 1e-30)
        exponent = jnp.floor(jnp.log2(largest)) + 2.0
        ref[pl.ds(k * rows, rows), :] = jnp.round(plane * jnp.exp2(15.0 - exponent)).astype(jnp.int32).astype(jnp.int16)
        exponents = jnp.where(place == k, exponent.astype(jnp.int32), exponents)
    ref[pl.ds(len(planes) * rows, 16), :] = exponents.astype(jnp.int16)


def load_scales(ref):
    exponents = ref[pl.ds(ref.shape[0] - 16, 16), :].astype(jnp.int32).astype(F32)
    return jnp.exp2(exponents - 15.0)


def load_edge(ref, scales, k, start, count):
    rows = (ref.shape[0] - 16) // 4
    return ref[pl.ds(k * rows + start, count), :].astype(jnp.int32).astype(F32) * scales[k : k + 1]


def edge(ref, near, far, near_part, far_part):
    store_edge(ref, (NEAR * near + FAR * far, near, NEAR * near_part + FAR * far_part, near_part))


def local_kernel(field_ref, potential_ref, part_ref, low_ref, high_ref):
    planes, rows, _ = part_ref.shape
    for z in range(planes):
        for start in range(0, rows, ROWS):
            part_ref[z, pl.ds(start, ROWS)] = stencil(field_ref, potential_ref, z, start, ROWS)
    edge(low_ref, field_ref[0], field_ref[1], part_ref[0], part_ref[1])
    edge(high_ref, field_ref[3], field_ref[2], part_ref[3], part_ref[2])


def member(place, size, first):
    return (first + place) % size


def fold(product):
    folded = jnp.sum(product.reshape(-1, 8, product.shape[-1]), axis=0)
    return folded[:, :128] + folded[:, 128:]


def product_rows(rounded_ref, partners_ref, out_ref):
    count, planes, rows, _ = partners_ref.shape
    totals = [jnp.zeros((8, 128), F32)] * count
    for z in range(planes):
        for start in range(0, rows, ROWS):
            rounded = rounded_ref[z, pl.ds(start, ROWS)].astype(F32)
            for k in range(count):
                totals[k] = totals[k] + fold(rounded * partners_ref[k, z, pl.ds(start, ROWS)].astype(F32))
    for k, total in enumerate(totals):
        out_ref[pl.ds(k, 1), :] = jnp.sum(total, axis=0, keepdims=True)


def filter_kernel(
    field_ref, potential_ref, part_ref, left_ref, right_ref, partners_ref, filtered_hbm, rounded_ref, rows_ref, first_ref, filtered_ref, sems
):
    planes, rows, _ = part_ref.shape
    sides = (left_ref, load_scales(left_ref), 0, 1), (right_ref, load_scales(right_ref), 3, 2)
    for ref, scales, near, far in sides:
        for start in range(0, rows, ROWS):
            block = pl.ds(start, ROWS)
            first_ref[near, block] = part_ref[near, block] + load_edge(ref, scales, 0, start, ROWS)
            first_ref[far, block] = part_ref[far, block] + FAR * load_edge(ref, scales, 1, start, ROWS)
    totals = [jnp.zeros((8, 128), F32)] * partners_ref.shape[0]
    copies = []
    for ref, scales, nearest, second in sides:
        for z in (nearest, second):
            for start in range(0, rows, ROWS):
                block = pl.ds(start, ROWS)
                value = stencil(first_ref, potential_ref, z, start, ROWS)
                f0, f1 = field_ref[nearest, block], field_ref[second, block]
                if z == nearest:
                    value = value + (load_edge(ref, scales, 2, start, ROWS) + ((NEAR * NEAR + FAR * FAR) * f0 + (NEAR * FAR) * f1))
                else:
                    value = value + FAR * (load_edge(ref, scales, 3, start, ROWS) + (NEAR * f0 + FAR * f1))
                filtered = 2.0 * value - (f0 if z == nearest else f1)
                filtered_ref[z, block] = filtered
                rounded = filtered.astype(BF16)
                rounded_ref[z, block] = rounded
                rounded = rounded.astype(F32)
                for k in range(len(totals)):
                    totals[k] = totals[k] + fold(rounded * partners_ref[k, z, block].astype(F32))
            copy = pltpu.make_async_copy(filtered_ref.at[z], filtered_hbm.at[z], sems.at[z])
            copy.start()
            copies.append(copy)
    for k, total in enumerate(totals):
        rows_ref[pl.ds(k, 1), :] = jnp.sum(total, axis=0, keepdims=True)
    for copy in copies:
        copy.wait()


def products_kernel(rounded_ref, partners_ref, own_ref, out_ref, other_ref):
    product_rows(rounded_ref, partners_ref, other_ref)
    core = lax.axis_index("core")
    own, other = own_ref[...], other_ref[...]
    rows = jnp.where(core == 0, own, other), jnp.where(core == 0, other, own)
    for place in range(out_ref.shape[0]):
        device = member(place, out_ref.shape[0], LAYER_FIRST)
        y = (device // 2 - Y_FIRST) % 4
        out_ref[pl.ds(place, 1), :] = rows[device % 2][y : y + 1]


def owners_kernel(places_ref, parts_ref, out_ref):
    totals = [jnp.zeros((1, 128), F32)] * ORBS
    for place in range(parts_ref.shape[0]):
        owner = member(place, parts_ref.shape[0], LAYER_FIRST) % ORBS
        totals[owner] = totals[owner] + parts_ref[pl.ds(place, 1), :]
    places = places_ref[...]
    chosen = jnp.zeros(places.shape, F32)
    for owner in range(ORBS):
        chosen = jnp.where(places == owner, totals[owner], chosen)
    sums = jnp.sum(chosen, axis=1, keepdims=True)
    row = lax.broadcasted_iota(jnp.int32, chosen.shape, 0)
    lane = lax.broadcasted_iota(jnp.int32, chosen.shape, 1)
    line = jnp.sum(jnp.where(row == lane, sums, 0.0), axis=0, keepdims=True)
    out_ref[...] = jnp.broadcast_to(line, out_ref.shape)


def last_kernel(parts_ref, out_ref):
    out_ref[...] = jnp.sum(parts_ref[...], axis=0, keepdims=True)[:, :STEPS] * FACTOR


def call(kernel, shapes, args, spaces=None, scratch=(), cost=None, out_spaces=None):
    spaces = spaces or [VMEM] * len(args)
    return pl.pallas_call(
        kernel,
        out_shape=shapes,
        in_specs=[pl.BlockSpec(memory_space=space) for space in spaces],
        out_specs=[pl.BlockSpec(memory_space=space) for space in out_spaces or [VMEM] * len(shapes)],
        scratch_shapes=list(scratch),
        compiler_params=pltpu.CompilerParams(vmem_limit_bytes=8 * 1024 * 1024),
        cost_estimate=cost,
    )(*args)


def from_middle(size, first):
    return [[(first + i) % size for i in range(size)]]


def shards(orbitals, potential, partners, owners):
    grid = ("z", "x")
    count = lax.axis_size(grid)
    up = [(i, (i + 1) % count) for i in range(count)]
    down = [(i, (i - 1) % count) for i in range(count)]
    _, planes, rows, columns = orbitals.shape
    shape = jax.ShapeDtypeStruct
    slab, edges = shape((planes, rows, columns), F32), shape((4 * rows + 16, columns), jnp.int16)

    copies = jnp.broadcast_to(partners, (4,) + partners.shape[1:])
    copies, orbitals = lax.optimization_barrier((copies, orbitals))
    partners = lax.all_to_all(copies, "y", 0, 0, tiled=True, axis_index_groups=from_middle(4, Y_FIRST))
    part, low, high = call(local_kernel, (slab, edges, edges), (orbitals[0], potential))
    left = lax.ppermute(high, grid, up)
    right = lax.ppermute(low, grid, down)
    owners, left = lax.optimization_barrier((owners, left))
    places = jnp.broadcast_to(jnp.pad(owners, (0, ORBS - STEPS), constant_values=ORBS)[:, None], (ORBS, 128))
    partners, places = lax.optimization_barrier((partners, places))
    others = lax.ppermute(partners, "core", [(0, 1), (1, 0)])
    filtered, rounded, own = call(
        filter_kernel,
        (slab, shape(slab.shape, BF16), shape((4, 128), F32)),
        (orbitals[0], potential, part, left, right, partners),
        scratch=(pltpu.VMEM(slab.shape, F32), pltpu.VMEM(slab.shape, F32), pltpu.SemaphoreType.DMA((planes,))),
        cost=pl.CostEstimate(flops=10**10, bytes_accessed=10**6, transcendentals=0),
        out_spaces=(pl.ANY, VMEM, VMEM),
    )
    parts = call(products_kernel, (shape((4 * ORBS, 128), F32),), (rounded, others, own), scratch=(pltpu.VMEM((4, 128), F32),))[0]
    layer = ("x", "y", "core")
    parts = lax.all_to_all(parts, layer, 0, 0, tiled=True, axis_index_groups=from_middle(4 * ORBS, LAYER_FIRST))
    depth = lax.axis_size("z")
    parts = call(owners_kernel, (shape((depth, 128), F32),), (places, parts))[0]
    parts = lax.all_to_all(parts, "z", 0, 0, tiled=True, axis_index_groups=from_middle(depth, Z_FIRST))
    intersection = call(last_kernel, (shape((1, STEPS), F32),), (parts,))[0]
    return filtered[None], intersection.T


def solution(mesh):
    fine = Mesh(mesh.devices.reshape(16, 4, 4, 2), ("z", "x", "y", "core"))
    grid, band = ("z", "x"), ("y", "core")
    in_specs = (P(band, grid, None, None), P(grid, None, None), P(band, grid, None, None), P())
    out_specs = (P(band, grid, None, None), P(None, band))
    return jax.shard_map(shards, mesh=fine, in_specs=in_specs, out_specs=out_specs, check_vma=False)
```

time: 59.6 us -> 58.9 us (0.988)
  waiting for transfers between devices: 4.09 us -> 6.34 us
  starting transfers between devices: 16.6 us -> 15.3 us
  blocking collectives: 32.1 us -> 30.9 us
    all_to_all x1, starting transfers between devices: 6.81 us -> 4.59 us  [shards(): lax.all_to_all(copies, 'y', 0, 0, tiled=True, axis_index_groups=from_midd...]
    all_to_all x1, blocking collectives: 17.3 us -> 15.5 us  [shards(): lax.all_to_all(parts, layer, 0, 0, tiled=True, axis_index_groups=from_mid...]
    all_to_all x1, waiting for transfers between devices: 1.21 us -> 2.97 us  [shards(): lax.all_to_all(copies, 'y', 0, 0, tiled=True, axis_index_groups=from_midd...]
    ppermute x1, starting transfers between devices: 4.46 us -> 5.41 us  [shards(): right = lax.ppermute(low, grid, down)]
    all_to_all x1, blocking collectives: 14.7 us -> 15.4 us  [shards(): lax.all_to_all(parts, 'z', 0, 0, tiled=True, axis_index_groups=from_middl...]
  transfers between devices with their start and end apart: 4 -> 4, of which waited for: 3 -> 3; matrix products, arithmetic and copies ran while one was open for 0% -> 0% of each run, Pallas kernels for 5% -> 4%
where the time goes in v4:
time: 58.9 us; the launch traced here: 58.6 us
  blocking collectives  30.9 us (52%)
  starting transfers between devices  15.3 us (26%)
  waiting for transfers between devices  6.34 us (11%)
  Pallas kernels  3.26 us (6%)
  local copies, waits for them, and re-layouts  2.1 us (4%)
  between operations  0.69 us (1%)
    all_to_all x1, blocking collectives, shards(): lax.all_to_all(parts, layer, 0, 0, tiled=True, axis_index_groups=from_mid...  15.5 us
    all_to_all x1, blocking collectives, shards(): lax.all_to_all(parts, 'z', 0, 0, tiled=True, axis_index_groups=from_middl...  15.4 us
    ppermute x1, starting transfers between devices, shards(): right = lax.ppermute(low, grid, down)  5.41 us
    all_to_all x1, starting transfers between devices, shards(): lax.all_to_all(copies, 'y', 0, 0, tiled=True, axis_index_groups=from_midd...  4.59 us
    ppermute x1, starting transfers between devices, shards(): left = lax.ppermute(high, grid, up)  3.4 us
    pallas_call x5, Pallas kernels, call(): pl.pallas_call(kernel, out_shape=shapes, in_specs=[pl.BlockSpec(memory_sp...  3.26 us
    all_to_all x1, waiting for transfers between devices, shards(): lax.all_to_all(copies, 'y', 0, 0, tiled=True, axis_index_groups=from_midd...  2.97 us
    ppermute x1, waiting for transfers between devices, shards(): left = lax.ppermute(high, grid, up)  2.5 us
  transfers between devices with their start and end apart: 4, of which 3 were waited for; matrix products, arithmetic and copies ran while one was open for 0% of the time, Pallas kernels for 4%

profile of v4, /device:TPU:2, one launch (start us, length us, event | category | flops | bytes accessed | tf_op | source)
XLA Modules:
  0.0 58.6 jit_solution(9134844848699053224)
XLA Ops:
  0.6 2.0 %broadcast_in_dim.17 = bf16[4,4,128,256]{3,2,1,0:T(8,128)(2,1)} broadcast(bf16[4,128,256]{2,1,0:T(8,128)(2,1)} %bitcast.18), dimensions={1,2,3} | broadcast | bytes 1310720 | tf_op jit(solution)/shard_map/broadcast_in_dim | solution.py:208
  2.6 0.0 copy-start
  2.6 0.0 copy-start.1
  2.7 4.6 %all-to-all-start = ((bf16[4,4,128,256]{3,2,1,0:T(8,128)(2,1)}), bf16[4,4,128,256]{3,2,1,0:T(8,128)(2,1)S(1)}, u32[]{:S(2)}, u32[]{:S(2)}) async-start(bf16[4,4,128,256]{3,2,1,0:T(8,128)(2,1)} %broadcast_in_dim.17), calls=%async_computation | async-start | bytes 2097152 | tf_op jit(solution)/shard_map/all_to_all | solution.py:210
  7.2 0.0 copy-done
  7.2 0.0 copy-done.1
  7.3 0.8 %shard_map.59 = (f32[4,128,256]{2,1,0:T(8,128)S(1)}, s16[528,256]{1,0:T(8,128)(2,1)S(1)}, s16[528,256]{1,0:T(8,128)(2,1)S(1)}) custom-call(f32[4,128,256]{2,1,0:T(8,128)S(1)} %bitcast.12, f32[4,128,256]{2,1,0:T(8,128)S(1)} %copy-done.1), custom_call_target="tpu_custom_call" | custom-call | tf_op jit(solution)/shard_map/pallas_call | solution.py:184
  8.0 0.0 copy-start.2
  8.0 3.4 %collective-permute-start = (s16[528,256]{1,0:T(8,128)(2,1)S(1)}, s16[528,256]{1,0:T(8,128)(2,1)S(1)}, u32[]{:S(2)}, u32[]{:S(2)}) collective-permute-start(s16[528,256]{1,0:T(8,128)(2,1)S(1)} %get-tuple-element.16), channel_id=1, source_target_pairs={{0,8},{8,16},{16,24},{24,32},{32,40},{40,48},{48,56},{56,64},{64,7... | collective-permute-start | bytes 811016 | tf_op jit(solution)/shard_map/ppermute | solution.py:212
  11.4 5.4 %collective-permute-start.1 = (s16[528,256]{1,0:T(8,128)(2,1)S(1)}, s16[528,256]{1,0:T(8,128)(2,1)S(1)}, u32[]{:S(2)}, u32[]{:S(2)}) collective-permute-start(s16[528,256]{1,0:T(8,128)(2,1)S(1)} %get-tuple-element.18), channel_id=1, source_target_pairs={{0,504},{8,0},{16,8},{24,16},{32,24},{40,32},{48,40},{56,48},{64,5... | collective-permute-start | bytes 811016 | tf_op jit(solution)/shard_map/ppermute | solution.py:213
  16.9 2.5 %collective-permute-done.left_ref = s16[528,256]{1,0:T(8,128)(2,1)S(1)} collective-permute-done((s16[528,256]{1,0:T(8,128)(2,1)S(1)}, s16[528,256]{1,0:T(8,128)(2,1)S(1)}, u32[]{:S(2)}, u32[]{:S(2)}) %collective-permute-start) | collective-permute-done | bytes 270368 | tf_op jit(solution)/shard_map/ppermute | solution.py:212
  19.4 0.0 copy-done.2
  19.4 3.0 %all-to-all-done.partners_ref = bf16[4,4,128,256]{3,2,1,0:T(8,128)(2,1)S(1)} async-done(((bf16[4,4,128,256]{3,2,1,0:T(8,128)(2,1)}), bf16[4,4,128,256]{3,2,1,0:T(8,128)(2,1)S(1)}, u32[]{:S(2)}, u32[]{:S(2)}) %all-to-all-start) | async-done | bytes 1048608 | tf_op jit(solution)/shard_map/all_to_all | solution.py:210
  22.3 0.1 broadcast_in_dim.18.places_ref
  22.4 1.9 %collective-permute-start.2 = (bf16[4,4,128,256]{3,2,1,0:T(8,128)(2,1)S(1)}, bf16[4,4,128,256]{3,2,1,0:T(8,128)(2,1)S(1)}, u32[]{:S(2)}, u32[]{:S(2)}) collective-permute-start(bf16[4,4,128,256]{3,2,1,0:T(8,128)(2,1)S(1)} %all-to-all-done.partners_ref), channel_id=1, source_target_pairs={{0,1},{1,0},{2,3},{3,2},{4,5},{5,4},{6,7},{7,6},{8,9},{9,8},{10,11... | collective-permute-start | bytes 3145736 | tf_op jit(solution)/shard_map/ppermute | solution.py:217
  24.3 0.0 collective-permute-done.1.right_ref
  24.3 1.7 %shard_map.60 = (f32[4,128,256]{2,1,0:T(8,128)}, bf16[4,128,256]{2,1,0:T(8,128)(2,1)S(1)}, f32[4,128]{1,0:T(4,128)S(1)}) custom-call(f32[4,128,256]{2,1,0:T(8,128)S(1)} %bitcast.13, f32[4,128,256]{2,1,0:T(8,128)S(1)} %copy-done.1, f32[4,128,256]{2,1,0:T(8,128)S(1)} %get-tuple-element.15.part_ref, s16[528,256]{1,0:T(8,128)(2,1)S(1)} %collective-permute-done.left_ref, ...), custom_call_target="tpu_custom_call" | custom-call | flops 10000000000 | bytes 1000000 | tf_op jit(solution)/shard_map/pallas_call | solution.py:184
  26.1 0.9 %collective-permute-done.2.partners_ref = bf16[4,4,128,256]{3,2,1,0:T(8,128)(2,1)S(1)} collective-permute-done((bf16[4,4,128,256]{3,2,1,0:T(8,128)(2,1)S(1)}, bf16[4,4,128,256]{3,2,1,0:T(8,128)(2,1)S(1)}, u32[]{:S(2)}, u32[]{:S(2)}) %collective-permute-start.2) | collective-permute-done | bytes 1048608 | tf_op jit(solution)/shard_map/ppermute | solution.py:217
  27.0 0.1 shard_map.61
  27.1 15.5 %all_to_all.27 = f32[32,1,128]{2,1,0:T(1,128)S(1)} all-to-all(f32[32,1,128]{2,1,0:T(1,128)S(1)} %bitcast.15), channel_id=1, replica_groups={{21,22,23,24,25,26,27,28,29,30,31,0,1,2,3,4,5,6,7,8,9,10,11,12,13,14,15..., dimensions={0} | all-to-all | bytes 32768 | tf_op jit(solution)/shard_map/all_to_all | solution.py:228
  42.6 0.1 shard_map.62
  42.7 15.4 %all_to_all.28 = f32[16,1,128]{2,1,0:T(1,128)S(1)} all-to-all(f32[16,1,128]{2,1,0:T(1,128)S(1)} %bitcast.16), channel_id=1, replica_groups={{256,288,320,352,384,416,448,480,0,32,64,96,128,160,192,224},{257,289,3..., dimensions={0} | all-to-all | bytes 16384 | tf_op jit(solution)/shard_map/all_to_all | solution.py:231
  58.0 0.5 shard_map.63
  (1 shorter events, 0.0 us)
Async XLA Ops:
  2.6 4.6 %copy-start = (f32[1,4,128,256]{3,2,1,0:T(8,128)S(1)}, f32[1,4,128,256]{3,2,1,0:T(8,128)}, u32[]{:S(2)}) copy-start(f32[1,4,128,256]{3,2,1,0:T(8,128)} %param.4) | copy-start | bytes 1572868
  2.6 4.6 %copy-start.1 = (f32[4,128,256]{2,1,0:T(8,128)S(1)}, f32[4,128,256]{2,1,0:T(8,128)}, u32[]{:S(2)}) copy-start(f32[4,128,256]{2,1,0:T(8,128)} %potential_ref.3) | copy-start | bytes 1572868
  2.7 19.7 %all-to-all-start = ((bf16[4,4,128,256]{3,2,1,0:T(8,128)(2,1)}), bf16[4,4,128,256]{3,2,1,0:T(8,128)(2,1)S(1)}, u32[]{:S(2)}, u32[]{:S(2)}) async-start(bf16[4,4,128,256]{3,2,1,0:T(8,128)(2,1)} %broadcast_in_dim.17), calls=%async_computation | async-start | bytes 2097152 | tf_op jit(solution)/shard_map/all_to_all | solution.py:210
  8.0 11.3 %copy-start.2 = (s32[6]{0:T(128)S(1)}, s32[6]{0:T(128)}, u32[]{:S(2)}) copy-start(s32[6]{0:T(128)} %param.7) | copy-start | bytes 76
  8.0 11.3 %collective-permute-start = (s16[528,256]{1,0:T(8,128)(2,1)S(1)}, s16[528,256]{1,0:T(8,128)(2,1)S(1)}, u32[]{:S(2)}, u32[]{:S(2)}) collective-permute-start(s16[528,256]{1,0:T(8,128)(2,1)S(1)} %get-tuple-element.16), channel_id=1, source_target_pairs={{0,8},{8,16},{16,24},{24,32},{32,40},{40,48},{48,56},{56,64},{64,7... | collective-permute-start | bytes 811016 | tf_op jit(solution)/shard_map/ppermute | solution.py:212
  11.4 12.9 %collective-permute-start.1 = (s16[528,256]{1,0:T(8,128)(2,1)S(1)}, s16[528,256]{1,0:T(8,128)(2,1)S(1)}, u32[]{:S(2)}, u32[]{:S(2)}) collective-permute-start(s16[528,256]{1,0:T(8,128)(2,1)S(1)} %get-tuple-element.18), channel_id=1, source_target_pairs={{0,504},{8,0},{16,8},{24,16},{32,24},{40,32},{48,40},{56,48},{64,5... | collective-permute-start | bytes 811016 | tf_op jit(solution)/shard_map/ppermute | solution.py:213
  22.4 4.5 %collective-permute-start.2 = (bf16[4,4,128,256]{3,2,1,0:T(8,128)(2,1)S(1)}, bf16[4,4,128,256]{3,2,1,0:T(8,128)(2,1)S(1)}, u32[]{:S(2)}, u32[]{:S(2)}) collective-permute-start(bf16[4,4,128,256]{3,2,1,0:T(8,128)(2,1)S(1)} %all-to-all-done.partners_ref), channel_id=1, source_target_pairs={{0,1},{1,0},{2,3},{3,2},{4,5},{5,4},{6,7},{7,6},{8,9},{9,8},{10,11... | collective-permute-start | bytes 3145736 | tf_op jit(solution)/shard_map/ppermute | solution.py:217

commit v5 on v4

--- a/solution.py
+++ b/solution.py
@@ -211,9 +211,9 @@
     part, low, high = call(local_kernel, (slab, edges, edges), (orbitals[0], potential))
     left = lax.ppermute(high, grid, up)
     right = lax.ppermute(low, grid, down)
-    owners, left = lax.optimization_barrier((owners, left))
+    owners, right = lax.optimization_barrier((owners, right))
     places = jnp.broadcast_to(jnp.pad(owners, (0, ORBS - STEPS), constant_values=ORBS)[:, None], (ORBS, 128))
-    partners, places = lax.optimization_barrier((partners, places))
+    partners, left = lax.optimization_barrier((partners, left))
     others = lax.ppermute(partners, "core", [(0, 1), (1, 0)])
     filtered, rounded, own = call(
         filter_kernel,
@@ -223,6 +223,7 @@
         cost=pl.CostEstimate(flops=10**10, bytes_accessed=10**6, transcendentals=0),
         out_spaces=(pl.ANY, VMEM, VMEM),
     )
+    rounded, places = lax.optimization_barrier((rounded, places))
     parts = call(products_kernel, (shape((4 * ORBS, 128), F32),), (rounded, others, own), scratch=(pltpu.VMEM((4, 128), F32),))[0]
     layer = ("x", "y", "core")
     parts = lax.all_to_all(parts, layer, 0, 0, tiled=True, axis_index_groups=from_middle(4 * ORBS, LAYER_FIRST))

time: 58.9 us -> 58.9 us (level)
  no operation moved by 1% of the time
where the time goes in v5:
time: 58.9 us; the launch traced here: 58.5 us
  blocking collectives  30.9 us (52%)
  starting transfers between devices  15.3 us (26%)
  waiting for transfers between devices  6.25 us (11%)
  Pallas kernels  3.26 us (6%)
  local copies, waits for them, and re-layouts  2.1 us (4%)
  between operations  0.71 us (1%)
    all_to_all x1, blocking collectives, shards(): lax.all_to_all(parts, layer, 0, 0, tiled=True, axis_index_groups=from_mid...  15.5 us
    all_to_all x1, blocking collectives, shards(): lax.all_to_all(parts, 'z', 0, 0, tiled=True, axis_index_groups=from_middl...  15.4 us
    ppermute x1, starting transfers between devices, shards(): right = lax.ppermute(low, grid, down)  5.41 us
    all_to_all x1, starting transfers between devices, shards(): lax.all_to_all(copies, 'y', 0, 0, tiled=True, axis_index_groups=from_midd...  4.59 us
    ppermute x1, starting transfers between devices, shards(): left = lax.ppermute(high, grid, up)  3.4 us
    pallas_call x5, Pallas kernels, call(): pl.pallas_call(kernel, out_shape=shapes, in_specs=[pl.BlockSpec(memory_sp...  3.26 us
    all_to_all x1, waiting for transfers between devices, shards(): lax.all_to_all(copies, 'y', 0, 0, tiled=True, axis_index_groups=from_midd...  2.98 us
    ppermute x1, waiting for transfers between devices, shards(): left = lax.ppermute(high, grid, up)  2.5 us
  transfers between devices with their start and end apart: 4, of which 3 were waited for; matrix products, arithmetic and copies ran while one was open for 0% of the time, Pallas kernels for 4%

profile of v5, /device:TPU:2, one launch (start us, length us, event | category | flops | bytes accessed | tf_op | source)
XLA Modules:
  0.0 58.5 jit_solution(16495261225083458111)
XLA Ops:
  0.6 2.0 %broadcast_in_dim.17 = bf16[4,4,128,256]{3,2,1,0:T(8,128)(2,1)} broadcast(bf16[4,128,256]{2,1,0:T(8,128)(2,1)} %bitcast.18), dimensions={1,2,3} | broadcast | bytes 1310720 | tf_op jit(solution)/shard_map/broadcast_in_dim | solution.py:208
  2.6 0.0 copy-start
  2.6 0.0 copy-start.1
  2.7 4.6 %all-to-all-start = ((bf16[4,4,128,256]{3,2,1,0:T(8,128)(2,1)}), bf16[4,4,128,256]{3,2,1,0:T(8,128)(2,1)S(1)}, u32[]{:S(2)}, u32[]{:S(2)}) async-start(bf16[4,4,128,256]{3,2,1,0:T(8,128)(2,1)} %broadcast_in_dim.17), calls=%async_computation | async-start | bytes 2097152 | tf_op jit(solution)/shard_map/all_to_all | solution.py:210
  7.2 0.0 copy-done
  7.2 0.0 copy-done.1
  7.3 0.8 %shard_map.59 = (f32[4,128,256]{2,1,0:T(8,128)S(1)}, s16[528,256]{1,0:T(8,128)(2,1)S(1)}, s16[528,256]{1,0:T(8,128)(2,1)S(1)}) custom-call(f32[4,128,256]{2,1,0:T(8,128)S(1)} %bitcast.12, f32[4,128,256]{2,1,0:T(8,128)S(1)} %copy-done.1), custom_call_target="tpu_custom_call" | custom-call | tf_op jit(solution)/shard_map/pallas_call | solution.py:184
  8.0 0.0 copy-start.2
  8.0 3.4 %collective-permute-start = (s16[528,256]{1,0:T(8,128)(2,1)S(1)}, s16[528,256]{1,0:T(8,128)(2,1)S(1)}, u32[]{:S(2)}, u32[]{:S(2)}) collective-permute-start(s16[528,256]{1,0:T(8,128)(2,1)S(1)} %get-tuple-element.19), channel_id=1, source_target_pairs={{0,8},{8,16},{16,24},{24,32},{32,40},{40,48},{48,56},{56,64},{64,7... | collective-permute-start | bytes 811016 | tf_op jit(solution)/shard_map/ppermute | solution.py:212
  11.4 5.4 %collective-permute-start.1 = (s16[528,256]{1,0:T(8,128)(2,1)S(1)}, s16[528,256]{1,0:T(8,128)(2,1)S(1)}, u32[]{:S(2)}, u32[]{:S(2)}) collective-permute-start(s16[528,256]{1,0:T(8,128)(2,1)S(1)} %get-tuple-element.21), channel_id=1, source_target_pairs={{0,504},{8,0},{16,8},{24,16},{32,24},{40,32},{48,40},{56,48},{64,5... | collective-permute-start | bytes 811016 | tf_op jit(solution)/shard_map/ppermute | solution.py:213
  16.9 2.5 %collective-permute-done.left_ref = s16[528,256]{1,0:T(8,128)(2,1)S(1)} collective-permute-done((s16[528,256]{1,0:T(8,128)(2,1)S(1)}, s16[528,256]{1,0:T(8,128)(2,1)S(1)}, u32[]{:S(2)}, u32[]{:S(2)}) %collective-permute-start) | collective-permute-done | bytes 270368 | tf_op jit(solution)/shard_map/ppermute | solution.py:212
  19.4 3.0 %all-to-all-done.partners_ref = bf16[4,4,128,256]{3,2,1,0:T(8,128)(2,1)S(1)} async-done(((bf16[4,4,128,256]{3,2,1,0:T(8,128)(2,1)}), bf16[4,4,128,256]{3,2,1,0:T(8,128)(2,1)S(1)}, u32[]{:S(2)}, u32[]{:S(2)}) %all-to-all-start) | async-done | bytes 1048608 | tf_op jit(solution)/shard_map/all_to_all | solution.py:210
  22.3 1.9 %collective-permute-start.2 = (bf16[4,4,128,256]{3,2,1,0:T(8,128)(2,1)S(1)}, bf16[4,4,128,256]{3,2,1,0:T(8,128)(2,1)S(1)}, u32[]{:S(2)}, u32[]{:S(2)}) collective-permute-start(bf16[4,4,128,256]{3,2,1,0:T(8,128)(2,1)S(1)} %all-to-all-done.partners_ref), channel_id=1, source_target_pairs={{0,1},{1,0},{2,3},{3,2},{4,5},{5,4},{6,7},{7,6},{8,9},{9,8},{10,11... | collective-permute-start | bytes 3145736 | tf_op jit(solution)/shard_map/ppermute | solution.py:217
  24.3 0.0 collective-permute-done.1.right_ref
  24.3 0.0 copy-done.2
  24.3 1.7 %shard_map.60 = (f32[4,128,256]{2,1,0:T(8,128)}, bf16[4,128,256]{2,1,0:T(8,128)(2,1)S(1)}, f32[4,128]{1,0:T(4,128)S(1)}) custom-call(f32[4,128,256]{2,1,0:T(8,128)S(1)} %bitcast.13, f32[4,128,256]{2,1,0:T(8,128)S(1)} %copy-done.1, f32[4,128,256]{2,1,0:T(8,128)S(1)} %get-tuple-element.17.part_ref, s16[528,256]{1,0:T(8,128)(2,1)S(1)} %collective-permute-done.left_ref, ...), custom_call_target="tpu_custom_call" | custom-call | flops 10000000000 | bytes 1000000 | tf_op jit(solution)/shard_map/pallas_call | solution.py:184
  26.0 0.1 broadcast_in_dim.19.places_ref
  26.1 0.8 %collective-permute-done.2.partners_ref = bf16[4,4,128,256]{3,2,1,0:T(8,128)(2,1)S(1)} collective-permute-done((bf16[4,4,128,256]{3,2,1,0:T(8,128)(2,1)S(1)}, bf16[4,4,128,256]{3,2,1,0:T(8,128)(2,1)S(1)}, u32[]{:S(2)}, u32[]{:S(2)}) %collective-permute-start.2) | collective-permute-done | bytes 1048608 | tf_op jit(solution)/shard_map/ppermute | solution.py:217
  26.9 0.1 shard_map.61
  27.0 15.5 %all_to_all.27 = f32[32,1,128]{2,1,0:T(1,128)S(1)} all-to-all(f32[32,1,128]{2,1,0:T(1,128)S(1)} %bitcast.15), channel_id=1, replica_groups={{21,22,23,24,25,26,27,28,29,30,31,0,1,2,3,4,5,6,7,8,9,10,11,12,13,14,15..., dimensions={0} | all-to-all | bytes 32768 | tf_op jit(solution)/shard_map/all_to_all | solution.py:229
  42.5 0.1 shard_map.62
  42.6 15.4 %all_to_all.28 = f32[16,1,128]{2,1,0:T(1,128)S(1)} all-to-all(f32[16,1,128]{2,1,0:T(1,128)S(1)} %bitcast.16), channel_id=1, replica_groups={{256,288,320,352,384,416,448,480,0,32,64,96,128,160,192,224},{257,289,3..., dimensions={0} | all-to-all | bytes 16384 | tf_op jit(solution)/shard_map/all_to_all | solution.py:232
  58.0 0.5 shard_map.63
  (1 shorter events, 0.0 us)
Async XLA Ops:
  2.6 4.6 %copy-start = (f32[1,4,128,256]{3,2,1,0:T(8,128)S(1)}, f32[1,4,128,256]{3,2,1,0:T(8,128)}, u32[]{:S(2)}) copy-start(f32[1,4,128,256]{3,2,1,0:T(8,128)} %param.4) | copy-start | bytes 1572868
  2.6 4.6 %copy-start.1 = (f32[4,128,256]{2,1,0:T(8,128)S(1)}, f32[4,128,256]{2,1,0:T(8,128)}, u32[]{:S(2)}) copy-start(f32[4,128,256]{2,1,0:T(8,128)} %potential_ref.3) | copy-start | bytes 1572868
  2.7 19.7 %all-to-all-start = ((bf16[4,4,128,256]{3,2,1,0:T(8,128)(2,1)}), bf16[4,4,128,256]{3,2,1,0:T(8,128)(2,1)S(1)}, u32[]{:S(2)}, u32[]{:S(2)}) async-start(bf16[4,4,128,256]{3,2,1,0:T(8,128)(2,1)} %broadcast_in_dim.17), calls=%async_computation | async-start | bytes 2097152 | tf_op jit(solution)/shard_map/all_to_all | solution.py:210
  8.0 16.2 %copy-start.2 = (s32[6]{0:T(128)S(1)}, s32[6]{0:T(128)}, u32[]{:S(2)}) copy-start(s32[6]{0:T(128)} %param.7) | copy-start | bytes 76
  8.0 11.3 %collective-permute-start = (s16[528,256]{1,0:T(8,128)(2,1)S(1)}, s16[528,256]{1,0:T(8,128)(2,1)S(1)}, u32[]{:S(2)}, u32[]{:S(2)}) collective-permute-start(s16[528,256]{1,0:T(8,128)(2,1)S(1)} %get-tuple-element.19), channel_id=1, source_target_pairs={{0,8},{8,16},{16,24},{24,32},{32,40},{40,48},{48,56},{56,64},{64,7... | collective-permute-start | bytes 811016 | tf_op jit(solution)/shard_map/ppermute | solution.py:212
  11.4 12.8 %collective-permute-start.1 = (s16[528,256]{1,0:T(8,128)(2,1)S(1)}, s16[528,256]{1,0:T(8,128)(2,1)S(1)}, u32[]{:S(2)}, u32[]{:S(2)}) collective-permute-start(s16[528,256]{1,0:T(8,128)(2,1)S(1)} %get-tuple-element.21), channel_id=1, source_target_pairs={{0,504},{8,0},{16,8},{24,16},{32,24},{40,32},{48,40},{56,48},{64,5... | collective-permute-start | bytes 811016 | tf_op jit(solution)/shard_map/ppermute | solution.py:213
  22.3 4.5 %collective-permute-start.2 = (bf16[4,4,128,256]{3,2,1,0:T(8,128)(2,1)S(1)}, bf16[4,4,128,256]{3,2,1,0:T(8,128)(2,1)S(1)}, u32[]{:S(2)}, u32[]{:S(2)}) collective-permute-start(bf16[4,4,128,256]{3,2,1,0:T(8,128)(2,1)S(1)} %all-to-all-done.partners_ref), channel_id=1, source_target_pairs={{0,1},{1,0},{2,3},{3,2},{4,5},{5,4},{6,7},{7,6},{8,9},{9,8},{10,11... | collective-permute-start | bytes 3145736 | tf_op jit(solution)/shard_map/ppermute | solution.py:217

commit v6 on v5

--- a/solution.py
+++ b/solution.py
@@ -52,6 +52,14 @@
         if 0 <= other < ref.shape[0]:
             far = far + ref[other, block]
     return (0.25 * (potential_ref[z, block] + DIAGONAL)) * center + (NEAR * near + FAR * far)
+
+
+def spread_kernel(source_ref, out_ref, sems):
+    copies = [pltpu.make_async_copy(source_ref, out_ref.at[k], sems.at[k]) for k in range(out_ref.shape[0])]
+    for copy in copies:
+        copy.start()
+    for copy in copies:
+        copy.wait()
 
 
 def store_edge(ref, planes):
@@ -205,8 +213,13 @@
     shape = jax.ShapeDtypeStruct
     slab, edges = shape((planes, rows, columns), F32), shape((4 * rows + 16, columns), jnp.int16)
 
-    copies = jnp.broadcast_to(partners, (4,) + partners.shape[1:])
-    copies, orbitals = lax.optimization_barrier((copies, orbitals))
+    copies = call(
+        spread_kernel,
+        (shape((4, planes, rows, columns), BF16),),
+        (partners[0],),
+        scratch=(pltpu.SemaphoreType.DMA((4,)),),
+        out_spaces=(pl.ANY,),
+    )[0]
     partners = lax.all_to_all(copies, "y", 0, 0, tiled=True, axis_index_groups=from_middle(4, Y_FIRST))
     part, low, high = call(local_kernel, (slab, edges, edges), (orbitals[0], potential))
     left = lax.ppermute(high, grid, up)

time: 58.9 us -> 58.8 us (level)
  local copies, waits for them, and re-layouts: 2.1 us -> 1.04 us
  Pallas kernels: 3.26 us -> 4.27 us
    broadcast_in_dim x1 -> x0, local copies, waits for them, and re-layouts: 2.02 us -> none  [shards(): copies = jnp.broadcast_to(partners, (4,) + partners.shape[1:])]
    pallas_call x5 -> x6, Pallas kernels: 3.26 us -> 4.27 us  [call(): pl.pallas_call(kernel, out_shape=shapes, in_specs=[pl.BlockSpec(memory_sp...]
    unnamed x6 -> x8, local copies, waits for them, and re-layouts: 0.01 us -> 0.96 us
where the time goes in v6:
time: 58.8 us; the launch traced here: 58.5 us
  blocking collectives  30.9 us (53%)
  starting transfers between devices  15.3 us (26%)
  waiting for transfers between devices  6.25 us (11%)
  Pallas kernels  4.27 us (7%)
  local copies, waits for them, and re-layouts  1.04 us (2%)
  between operations  0.74 us (1%)
    all_to_all x1, blocking collectives, shards(): lax.all_to_all(parts, layer, 0, 0, tiled=True, axis_index_groups=from_mid...  15.5 us
    all_to_all x1, blocking collectives, shards(): lax.all_to_all(parts, 'z', 0, 0, tiled=True, axis_index_groups=from_middl...  15.4 us
    ppermute x1, starting transfers between devices, shards(): right = lax.ppermute(low, grid, down)  5.41 us
    all_to_all x1, starting transfers between devices, shards(): lax.all_to_all(copies, 'y', 0, 0, tiled=True, axis_index_groups=from_midd...  4.61 us
    pallas_call x6, Pallas kernels, call(): pl.pallas_call(kernel, out_shape=shapes, in_specs=[pl.BlockSpec(memory_sp...  4.27 us
    ppermute x1, starting transfers between devices, shards(): left = lax.ppermute(high, grid, up)  3.4 us
    all_to_all x1, waiting for transfers between devices, shards(): lax.all_to_all(copies, 'y', 0, 0, tiled=True, axis_index_groups=from_midd...  2.98 us
    ppermute x1, waiting for transfers between devices, shards(): left = lax.ppermute(high, grid, up)  2.5 us
  transfers between devices with their start and end apart: 4, of which 3 were waited for; matrix products, arithmetic and copies ran while one was open for 0% of the time, Pallas kernels for 4%

profile of v6, /device:TPU:2, one launch (start us, length us, event | category | flops | bytes accessed | tf_op | source)
XLA Modules:
  0.0 58.5 jit_solution(602617010060760344)
XLA Ops:
  0.6 0.0 copy-start.2
  0.6 0.9 %copy-done.2 = bf16[1,4,128,256]{3,2,1,0:T(8,128)(2,1)S(1)} copy-done((bf16[1,4,128,256]{3,2,1,0:T(8,128)(2,1)S(1)}, bf16[1,4,128,256]{3,2,1,0:T(8,128)(2,1)}, u32[]{:S(2)}) %copy-start.2) | copy-done | bytes 262168
  1.6 1.0 %shard_map.60 = bf16[4,4,128,256]{3,2,1,0:T(8,128)(2,1)} custom-call(bf16[4,128,256]{2,1,0:T(8,128)(2,1)S(1)} %bitcast.14), custom_call_target="tpu_custom_call" | custom-call | tf_op jit(solution)/shard_map/pallas_call | solution.py:192
  2.6 0.0 copy-start
  2.6 0.0 copy-start.1
  2.6 4.6 %all-to-all-start = ((bf16[4,4,128,256]{3,2,1,0:T(8,128)(2,1)}), bf16[4,4,128,256]{3,2,1,0:T(8,128)(2,1)S(1)}, u32[]{:S(2)}, u32[]{:S(2)}) async-start(bf16[4,4,128,256]{3,2,1,0:T(8,128)(2,1)} %shard_map.60), calls=%async_computation | async-start | bytes 2097152 | tf_op jit(solution)/shard_map/all_to_all | solution.py:223
  7.2 0.0 copy-done
  7.2 0.0 copy-done.1
  7.2 0.8 %shard_map.59 = (f32[4,128,256]{2,1,0:T(8,128)S(1)}, s16[528,256]{1,0:T(8,128)(2,1)S(1)}, s16[528,256]{1,0:T(8,128)(2,1)S(1)}) custom-call(f32[4,128,256]{2,1,0:T(8,128)S(1)} %bitcast.12, f32[4,128,256]{2,1,0:T(8,128)S(1)} %copy-done.1), custom_call_target="tpu_custom_call" | custom-call | tf_op jit(solution)/shard_map/pallas_call | solution.py:192
  8.0 0.0 copy-start.3
  8.0 3.4 %collective-permute-start = (s16[528,256]{1,0:T(8,128)(2,1)S(1)}, s16[528,256]{1,0:T(8,128)(2,1)S(1)}, u32[]{:S(2)}, u32[]{:S(2)}) collective-permute-start(s16[528,256]{1,0:T(8,128)(2,1)S(1)} %get-tuple-element.15), channel_id=1, source_target_pairs={{0,8},{8,16},{16,24},{24,32},{32,40},{40,48},{48,56},{56,64},{64,7... | collective-permute-start | bytes 811016 | tf_op jit(solution)/shard_map/ppermute | solution.py:225
  11.4 5.4 %collective-permute-start.1 = (s16[528,256]{1,0:T(8,128)(2,1)S(1)}, s16[528,256]{1,0:T(8,128)(2,1)S(1)}, u32[]{:S(2)}, u32[]{:S(2)}) collective-permute-start(s16[528,256]{1,0:T(8,128)(2,1)S(1)} %get-tuple-element.17), channel_id=1, source_target_pairs={{0,504},{8,0},{16,8},{24,16},{32,24},{40,32},{48,40},{56,48},{64,5... | collective-permute-start | bytes 811016 | tf_op jit(solution)/shard_map/ppermute | solution.py:226
  16.9 2.5 %collective-permute-done.left_ref = s16[528,256]{1,0:T(8,128)(2,1)S(1)} collective-permute-done((s16[528,256]{1,0:T(8,128)(2,1)S(1)}, s16[528,256]{1,0:T(8,128)(2,1)S(1)}, u32[]{:S(2)}, u32[]{:S(2)}) %collective-permute-start) | collective-permute-done | bytes 270368 | tf_op jit(solution)/shard_map/ppermute | solution.py:225
  19.3 3.0 %all-to-all-done.partners_ref = bf16[4,4,128,256]{3,2,1,0:T(8,128)(2,1)S(1)} async-done(((bf16[4,4,128,256]{3,2,1,0:T(8,128)(2,1)}), bf16[4,4,128,256]{3,2,1,0:T(8,128)(2,1)S(1)}, u32[]{:S(2)}, u32[]{:S(2)}) %all-to-all-start) | async-done | bytes 1048608 | tf_op jit(solution)/shard_map/all_to_all | solution.py:223
  22.3 1.9 %collective-permute-start.2 = (bf16[4,4,128,256]{3,2,1,0:T(8,128)(2,1)S(1)}, bf16[4,4,128,256]{3,2,1,0:T(8,128)(2,1)S(1)}, u32[]{:S(2)}, u32[]{:S(2)}) collective-permute-start(bf16[4,4,128,256]{3,2,1,0:T(8,128)(2,1)S(1)} %all-to-all-done.partners_ref), channel_id=1, source_target_pairs={{0,1},{1,0},{2,3},{3,2},{4,5},{5,4},{6,7},{7,6},{8,9},{9,8},{10,11... | collective-permute-start | bytes 3145736 | tf_op jit(solution)/shard_map/ppermute | solution.py:230
  24.2 0.0 collective-permute-done.1.right_ref
  24.3 0.0 copy-done.3
  24.3 1.7 %shard_map.61 = (f32[4,128,256]{2,1,0:T(8,128)}, bf16[4,128,256]{2,1,0:T(8,128)(2,1)S(1)}, f32[4,128]{1,0:T(4,128)S(1)}) custom-call(f32[4,128,256]{2,1,0:T(8,128)S(1)} %bitcast.13, f32[4,128,256]{2,1,0:T(8,128)S(1)} %copy-done.1, f32[4,128,256]{2,1,0:T(8,128)S(1)} %get-tuple-element.14.part_ref, s16[528,256]{1,0:T(8,128)(2,1)S(1)} %collective-permute-done.left_ref, ...), custom_call_target="tpu_custom_call" | custom-call | flops 10000000000 | bytes 1000000 | tf_op jit(solution)/shard_map/pallas_call | solution.py:192
  26.0 0.1 broadcast_in_dim.10.places_ref
  26.1 0.8 %collective-permute-done.2.partners_ref = bf16[4,4,128,256]{3,2,1,0:T(8,128)(2,1)S(1)} collective-permute-done((bf16[4,4,128,256]{3,2,1,0:T(8,128)(2,1)S(1)}, bf16[4,4,128,256]{3,2,1,0:T(8,128)(2,1)S(1)}, u32[]{:S(2)}, u32[]{:S(2)}) %collective-permute-start.2) | collective-permute-done | bytes 1048608 | tf_op jit(solution)/shard_map/ppermute | solution.py:230
  26.9 0.1 shard_map.62
  27.0 15.5 %all_to_all.27 = f32[32,1,128]{2,1,0:T(1,128)S(1)} all-to-all(f32[32,1,128]{2,1,0:T(1,128)S(1)} %bitcast.16), channel_id=1, replica_groups={{21,22,23,24,25,26,27,28,29,30,31,0,1,2,3,4,5,6,7,8,9,10,11,12,13,14,15..., dimensions={0} | all-to-all | bytes 32768 | tf_op jit(solution)/shard_map/all_to_all | solution.py:242
  42.5 0.1 shard_map.63
  42.6 15.4 %all_to_all.28 = f32[16,1,128]{2,1,0:T(1,128)S(1)} all-to-all(f32[16,1,128]{2,1,0:T(1,128)S(1)} %bitcast.17), channel_id=1, replica_groups={{256,288,320,352,384,416,448,480,0,32,64,96,128,160,192,224},{257,289,3..., dimensions={0} | all-to-all | bytes 16384 | tf_op jit(solution)/shard_map/all_to_all | solution.py:245
  58.0 0.5 shard_map.64
  (1 shorter events, 0.0 us)
Async XLA Ops:
  0.6 1.0 %copy-start.2 = (bf16[1,4,128,256]{3,2,1,0:T(8,128)(2,1)S(1)}, bf16[1,4,128,256]{3,2,1,0:T(8,128)(2,1)}, u32[]{:S(2)}) copy-start(bf16[1,4,128,256]{3,2,1,0:T(8,128)(2,1)} %param.6) | copy-start | bytes 786436
  2.6 4.6 %copy-start = (f32[1,4,128,256]{3,2,1,0:T(8,128)S(1)}, f32[1,4,128,256]{3,2,1,0:T(8,128)}, u32[]{:S(2)}) copy-start(f32[1,4,128,256]{3,2,1,0:T(8,128)} %param.4) | copy-start | bytes 1572868
  2.6 4.6 %copy-start.1 = (f32[4,128,256]{2,1,0:T(8,128)S(1)}, f32[4,128,256]{2,1,0:T(8,128)}, u32[]{:S(2)}) copy-start(f32[4,128,256]{2,1,0:T(8,128)} %potential_ref.3) | copy-start | bytes 1572868
  2.6 19.7 %all-to-all-start = ((bf16[4,4,128,256]{3,2,1,0:T(8,128)(2,1)}), bf16[4,4,128,256]{3,2,1,0:T(8,128)(2,1)S(1)}, u32[]{:S(2)}, u32[]{:S(2)}) async-start(bf16[4,4,128,256]{3,2,1,0:T(8,128)(2,1)} %shard_map.60), calls=%async_computation | async-start | bytes 2097152 | tf_op jit(solution)/shard_map/all_to_all | solution.py:223
  8.0 16.2 %copy-start.3 = (s32[6]{0:T(128)S(1)}, s32[6]{0:T(128)}, u32[]{:S(2)}) copy-start(s32[6]{0:T(128)} %param.7) | copy-start | bytes 76
  8.0 11.3 %collective-permute-start = (s16[528,256]{1,0:T(8,128)(2,1)S(1)}, s16[528,256]{1,0:T(8,128)(2,1)S(1)}, u32[]{:S(2)}, u32[]{:S(2)}) collective-permute-start(s16[528,256]{1,0:T(8,128)(2,1)S(1)} %get-tuple-element.15), channel_id=1, source_target_pairs={{0,8},{8,16},{16,24},{24,32},{32,40},{40,48},{48,56},{56,64},{64,7... | collective-permute-start | bytes 811016 | tf_op jit(solution)/shard_map/ppermute | solution.py:225
  11.4 12.8 %collective-permute-start.1 = (s16[528,256]{1,0:T(8,128)(2,1)S(1)}, s16[528,256]{1,0:T(8,128)(2,1)S(1)}, u32[]{:S(2)}, u32[]{:S(2)}) collective-permute-start(s16[528,256]{1,0:T(8,128)(2,1)S(1)} %get-tuple-element.17), channel_id=1, source_target_pairs={{0,504},{8,0},{16,8},{24,16},{32,24},{40,32},{48,40},{56,48},{64,5... | collective-permute-start | bytes 811016 | tf_op jit(solution)/shard_map/ppermute | solution.py:226
  22.3 4.5 %collective-permute-start.2 = (bf16[4,4,128,256]{3,2,1,0:T(8,128)(2,1)S(1)}, bf16[4,4,128,256]{3,2,1,0:T(8,128)(2,1)S(1)}, u32[]{:S(2)}, u32[]{:S(2)}) collective-permute-start(bf16[4,4,128,256]{3,2,1,0:T(8,128)(2,1)S(1)} %all-to-all-done.partners_ref), channel_id=1, source_target_pairs={{0,1},{1,0},{2,3},{3,2},{4,5},{5,4},{6,7},{7,6},{8,9},{9,8},{10,11... | collective-permute-start | bytes 3145736 | tf_op jit(solution)/shard_map/ppermute | solution.py:230

commit v7 on v6

--- a/solution.py
+++ b/solution.py
@@ -19,7 +19,7 @@
 F32 = jnp.float32
 BF16 = jnp.bfloat16
 
-ROWS = 32
+ROWS = 64
 
 Z_FIRST = 8
 LAYER_FIRST = 21

time: 58.8 us -> 58.8 us (level)
  no operation moved by 1% of the time
where the time goes in v7:
time: 58.8 us; the launch traced here: 58.4 us
  blocking collectives  30.9 us (53%)
  starting transfers between devices  15.3 us (26%)
  waiting for transfers between devices  6.2 us (11%)
  Pallas kernels  4.28 us (7%)
  local copies, waits for them, and re-layouts  1.04 us (2%)
  between operations  0.74 us (1%)
    all_to_all x1, blocking collectives, shards(): lax.all_to_all(parts, layer, 0, 0, tiled=True, axis_index_groups=from_mid...  15.5 us
    all_to_all x1, blocking collectives, shards(): lax.all_to_all(parts, 'z', 0, 0, tiled=True, axis_index_groups=from_middl...  15.3 us
    ppermute x1, starting transfers between devices, shards(): right = lax.ppermute(low, grid, down)  5.41 us
    all_to_all x1, starting transfers between devices, shards(): lax.all_to_all(copies, 'y', 0, 0, tiled=True, axis_index_groups=from_midd...  4.61 us
    pallas_call x6, Pallas kernels, call(): pl.pallas_call(kernel, out_shape=shapes, in_specs=[pl.BlockSpec(memory_sp...  4.28 us
    ppermute x1, starting transfers between devices, shards(): left = lax.ppermute(high, grid, up)  3.4 us
    all_to_all x1, waiting for transfers between devices, shards(): lax.all_to_all(copies, 'y', 0, 0, tiled=True, axis_index_groups=from_midd...  2.95 us
    ppermute x1, waiting for transfers between devices, shards(): left = lax.ppermute(high, grid, up)  2.5 us
  transfers between devices with their start and end apart: 4, of which 3 were waited for; matrix products, arithmetic and copies ran while one was open for 0% of the time, Pallas kernels for 4%

profile of v7, /device:TPU:2, one launch (start us, length us, event | category | flops | bytes accessed | tf_op | source)
XLA Modules:
  0.0 58.4 jit_solution(11982337143722947325)
XLA Ops:
  0.6 0.0 copy-start.2
  0.6 0.9 %copy-done.2 = bf16[1,4,128,256]{3,2,1,0:T(8,128)(2,1)S(1)} copy-done((bf16[1,4,128,256]{3,2,1,0:T(8,128)(2,1)S(1)}, bf16[1,4,128,256]{3,2,1,0:T(8,128)(2,1)}, u32[]{:S(2)}) %copy-start.2) | copy-done | bytes 262168
  1.6 1.0 %shard_map.60 = bf16[4,4,128,256]{3,2,1,0:T(8,128)(2,1)} custom-call(bf16[4,128,256]{2,1,0:T(8,128)(2,1)S(1)} %bitcast.14), custom_call_target="tpu_custom_call" | custom-call | tf_op jit(solution)/shard_map/pallas_call | solution.py:192
  2.6 0.0 copy-start
  2.6 0.0 copy-start.1
  2.6 4.6 %all-to-all-start = ((bf16[4,4,128,256]{3,2,1,0:T(8,128)(2,1)}), bf16[4,4,128,256]{3,2,1,0:T(8,128)(2,1)S(1)}, u32[]{:S(2)}, u32[]{:S(2)}) async-start(bf16[4,4,128,256]{3,2,1,0:T(8,128)(2,1)} %shard_map.60), calls=%async_computation | async-start | bytes 2097152 | tf_op jit(solution)/shard_map/all_to_all | solution.py:223
  7.2 0.0 copy-done
  7.2 0.0 copy-done.1
  7.2 0.8 %shard_map.59 = (f32[4,128,256]{2,1,0:T(8,128)S(1)}, s16[528,256]{1,0:T(8,128)(2,1)S(1)}, s16[528,256]{1,0:T(8,128)(2,1)S(1)}) custom-call(f32[4,128,256]{2,1,0:T(8,128)S(1)} %bitcast.12, f32[4,128,256]{2,1,0:T(8,128)S(1)} %copy-done.1), custom_call_target="tpu_custom_call" | custom-call | tf_op jit(solution)/shard_map/pallas_call | solution.py:192
  8.0 0.0 copy-start.3
  8.0 3.4 %collective-permute-start = (s16[528,256]{1,0:T(8,128)(2,1)S(1)}, s16[528,256]{1,0:T(8,128)(2,1)S(1)}, u32[]{:S(2)}, u32[]{:S(2)}) collective-permute-start(s16[528,256]{1,0:T(8,128)(2,1)S(1)} %get-tuple-element.15), channel_id=1, source_target_pairs={{0,8},{8,16},{16,24},{24,32},{32,40},{40,48},{48,56},{56,64},{64,7... | collective-permute-start | bytes 811016 | tf_op jit(solution)/shard_map/ppermute | solution.py:225
  11.5 5.4 %collective-permute-start.1 = (s16[528,256]{1,0:T(8,128)(2,1)S(1)}, s16[528,256]{1,0:T(8,128)(2,1)S(1)}, u32[]{:S(2)}, u32[]{:S(2)}) collective-permute-start(s16[528,256]{1,0:T(8,128)(2,1)S(1)} %get-tuple-element.17), channel_id=1, source_target_pairs={{0,504},{8,0},{16,8},{24,16},{32,24},{40,32},{48,40},{56,48},{64,5... | collective-permute-start | bytes 811016 | tf_op jit(solution)/shard_map/ppermute | solution.py:226
  16.9 2.5 %collective-permute-done.left_ref = s16[528,256]{1,0:T(8,128)(2,1)S(1)} collective-permute-done((s16[528,256]{1,0:T(8,128)(2,1)S(1)}, s16[528,256]{1,0:T(8,128)(2,1)S(1)}, u32[]{:S(2)}, u32[]{:S(2)}) %collective-permute-start) | collective-permute-done | bytes 270368 | tf_op jit(solution)/shard_map/ppermute | solution.py:225
  19.4 3.0 %all-to-all-done.partners_ref = bf16[4,4,128,256]{3,2,1,0:T(8,128)(2,1)S(1)} async-done(((bf16[4,4,128,256]{3,2,1,0:T(8,128)(2,1)}), bf16[4,4,128,256]{3,2,1,0:T(8,128)(2,1)S(1)}, u32[]{:S(2)}, u32[]{:S(2)}) %all-to-all-start) | async-done | bytes 1048608 | tf_op jit(solution)/shard_map/all_to_all | solution.py:223
  22.3 1.9 %collective-permute-start.2 = (bf16[4,4,128,256]{3,2,1,0:T(8,128)(2,1)S(1)}, bf16[4,4,128,256]{3,2,1,0:T(8,128)(2,1)S(1)}, u32[]{:S(2)}, u32[]{:S(2)}) collective-permute-start(bf16[4,4,128,256]{3,2,1,0:T(8,128)(2,1)S(1)} %all-to-all-done.partners_ref), channel_id=1, source_target_pairs={{0,1},{1,0},{2,3},{3,2},{4,5},{5,4},{6,7},{7,6},{8,9},{9,8},{10,11... | collective-permute-start | bytes 3145736 | tf_op jit(solution)/shard_map/ppermute | solution.py:230
  24.2 0.0 collective-permute-done.1.right_ref
  24.3 0.0 copy-done.3
  24.3 1.8 %shard_map.61 = (f32[4,128,256]{2,1,0:T(8,128)}, bf16[4,128,256]{2,1,0:T(8,128)(2,1)S(1)}, f32[4,128]{1,0:T(4,128)S(1)}) custom-call(f32[4,128,256]{2,1,0:T(8,128)S(1)} %bitcast.13, f32[4,128,256]{2,1,0:T(8,128)S(1)} %copy-done.1, f32[4,128,256]{2,1,0:T(8,128)S(1)} %get-tuple-element.14.part_ref, s16[528,256]{1,0:T(8,128)(2,1)S(1)} %collective-permute-done.left_ref, ...), custom_call_target="tpu_custom_call" | custom-call | flops 10000000000 | bytes 1000000 | tf_op jit(solution)/shard_map/pallas_call | solution.py:192
  26.0 0.1 broadcast_in_dim.10.places_ref
  26.1 0.7 %collective-permute-done.2.partners_ref = bf16[4,4,128,256]{3,2,1,0:T(8,128)(2,1)S(1)} collective-permute-done((bf16[4,4,128,256]{3,2,1,0:T(8,128)(2,1)S(1)}, bf16[4,4,128,256]{3,2,1,0:T(8,128)(2,1)S(1)}, u32[]{:S(2)}, u32[]{:S(2)}) %collective-permute-start.2) | collective-permute-done | bytes 1048608 | tf_op jit(solution)/shard_map/ppermute | solution.py:230
  26.9 0.1 shard_map.62
  27.0 15.5 %all_to_all.27 = f32[32,1,128]{2,1,0:T(1,128)S(1)} all-to-all(f32[32,1,128]{2,1,0:T(1,128)S(1)} %bitcast.16), channel_id=1, replica_groups={{21,22,23,24,25,26,27,28,29,30,31,0,1,2,3,4,5,6,7,8,9,10,11,12,13,14,15..., dimensions={0} | all-to-all | bytes 32768 | tf_op jit(solution)/shard_map/all_to_all | solution.py:242
  42.5 0.1 shard_map.63
  42.6 15.3 %all_to_all.28 = f32[16,1,128]{2,1,0:T(1,128)S(1)} all-to-all(f32[16,1,128]{2,1,0:T(1,128)S(1)} %bitcast.17), channel_id=1, replica_groups={{256,288,320,352,384,416,448,480,0,32,64,96,128,160,192,224},{257,289,3..., dimensions={0} | all-to-all | bytes 16384 | tf_op jit(solution)/shard_map/all_to_all | solution.py:245
  57.9 0.5 shard_map.64
  (1 shorter events, 0.0 us)
Async XLA Ops:
  0.6 1.0 %copy-start.2 = (bf16[1,4,128,256]{3,2,1,0:T(8,128)(2,1)S(1)}, bf16[1,4,128,256]{3,2,1,0:T(8,128)(2,1)}, u32[]{:S(2)}) copy-start(bf16[1,4,128,256]{3,2,1,0:T(8,128)(2,1)} %param.6) | copy-start | bytes 786436
  2.6 4.6 %copy-start = (f32[1,4,128,256]{3,2,1,0:T(8,128)S(1)}, f32[1,4,128,256]{3,2,1,0:T(8,128)}, u32[]{:S(2)}) copy-start(f32[1,4,128,256]{3,2,1,0:T(8,128)} %param.4) | copy-start | bytes 1572868
  2.6 4.6 %copy-start.1 = (f32[4,128,256]{2,1,0:T(8,128)S(1)}, f32[4,128,256]{2,1,0:T(8,128)}, u32[]{:S(2)}) copy-start(f32[4,128,256]{2,1,0:T(8,128)} %potential_ref.3) | copy-start | bytes 1572868
  2.6 19.7 %all-to-all-start = ((bf16[4,4,128,256]{3,2,1,0:T(8,128)(2,1)}), bf16[4,4,128,256]{3,2,1,0:T(8,128)(2,1)S(1)}, u32[]{:S(2)}, u32[]{:S(2)}) async-start(bf16[4,4,128,256]{3,2,1,0:T(8,128)(2,1)} %shard_map.60), calls=%async_computation | async-start | bytes 2097152 | tf_op jit(solution)/shard_map/all_to_all | solution.py:223
  8.0 16.2 %copy-start.3 = (s32[6]{0:T(128)S(1)}, s32[6]{0:T(128)}, u32[]{:S(2)}) copy-start(s32[6]{0:T(128)} %param.7) | copy-start | bytes 76
  8.0 11.3 %collective-permute-start = (s16[528,256]{1,0:T(8,128)(2,1)S(1)}, s16[528,256]{1,0:T(8,128)(2,1)S(1)}, u32[]{:S(2)}, u32[]{:S(2)}) collective-permute-start(s16[528,256]{1,0:T(8,128)(2,1)S(1)} %get-tuple-element.15), channel_id=1, source_target_pairs={{0,8},{8,16},{16,24},{24,32},{32,40},{40,48},{48,56},{56,64},{64,7... | collective-permute-start | bytes 811016 | tf_op jit(solution)/shard_map/ppermute | solution.py:225
  11.5 12.8 %collective-permute-start.1 = (s16[528,256]{1,0:T(8,128)(2,1)S(1)}, s16[528,256]{1,0:T(8,128)(2,1)S(1)}, u32[]{:S(2)}, u32[]{:S(2)}) collective-permute-start(s16[528,256]{1,0:T(8,128)(2,1)S(1)} %get-tuple-element.17), channel_id=1, source_target_pairs={{0,504},{8,0},{16,8},{24,16},{32,24},{40,32},{48,40},{56,48},{64,5... | collective-permute-start | bytes 811016 | tf_op jit(solution)/shard_map/ppermute | solution.py:226
  22.3 4.5 %collective-permute-start.2 = (bf16[4,4,128,256]{3,2,1,0:T(8,128)(2,1)S(1)}, bf16[4,4,128,256]{3,2,1,0:T(8,128)(2,1)S(1)}, u32[]{:S(2)}, u32[]{:S(2)}) collective-permute-start(bf16[4,4,128,256]{3,2,1,0:T(8,128)(2,1)S(1)} %all-to-all-done.partners_ref), channel_id=1, source_target_pairs={{0,1},{1,0},{2,3},{3,2},{4,5},{5,4},{6,7},{7,6},{8,9},{9,8},{10,11... | collective-permute-start | bytes 3145736 | tf_op jit(solution)/shard_map/ppermute | solution.py:230
